TPU v7x, 32 devices: a whole 2x2x4 slice. The times are simulated.
32 devices in a mesh: row: 4 (over y, core), col: 8 (over z, x).
Axes of the slice: x: 2, y: 2, z: 4, core: 2. Of those that a mesh axis runs over, the one named last changes fastest.
Arguments:
- x_paper: bfloat16 [8192, 768], P(('row', 'col')), may hold values from -6 to 6
- x_author: bfloat16 [8192, 768], P(('row', 'col')), may hold values from -6 to 6
- cite_nbr: int32 [8192, 16], P(('row', 'col')), may hold values from -1 to 2047, as said below
- write_src: int32 [32, 32, 4], P(('row', 'col')), may hold values from -1 to 255, as said below
- write_dst: int32 [32, 32, 4], P(('row', 'col')), may hold values from -1 to 255, as said below
- w_self_paper: bfloat16 [768, 1024], replicated, may hold values from -0.21875 to 0.21875
- w_cite: bfloat16 [768, 1024], replicated, may hold values from -0.21875 to 0.21875
- w_write: bfloat16 [768, 1024], replicated, may hold values from -0.21875 to 0.21875
- w_self_author: bfloat16 [768, 1024], replicated, may hold values from -0.21875 to 0.21875
- w_written: bfloat16 [768, 1024], replicated, may hold values from -0.21875 to 0.21875
- grad_paper: bfloat16 [8192, 1024], P(('row', 'col')), may hold values from -6 to 6
- grad_author: bfloat16 [8192, 1024], P(('row', 'col')), may hold values from -6 to 6
Outputs:
- out_paper: bfloat16 [8192, 1024], P(('row', 'col'))
- out_author: bfloat16 [8192, 1024], P(('row', 'col'))
- dx_paper: bfloat16 [8192, 768], P(('row', 'col'))
- dx_author: bfloat16 [8192, 768], P(('row', 'col'))
- dweights: float32 [5, 768, 1024], P(None, 'row', 'col')
Inputs may be any that keep to these rules, and one draw needn't show every extreme that they name: `cite_nbr`: entries of a row that are -1 stand for no citation and come after all others; a value e >= 0 names the paper at position e of the paper's own block row. Some paper has all 16 entries. write_src[s, d, j] is -1 (empty slot) exactly where write_dst[d, s, j] is -1; otherwise it is an author position on device s. Some device d has every slot from every device s filled. write_dst[d, s, j] is -1 exactly where write_src[s, d, j] is -1; otherwise it is a paper position on device d. A paper may have several edges, also from one author.
All inputs are finite; a program needn't handle non-finite values.
Results may differ from a plain program's by a relative error of at most 0.0054.
Values may be sent and summed in bfloat16 or wider, within the bound.
A program may use at most 192 MiB of HBM per device.

v0:
```python
import jax
import jax.numpy as jnp
from jax import lax
from jax.sharding import PartitionSpec as P


def match_table(entries, columns):
    accum = jnp.zeros((entries.shape[0], columns.shape[0]), jnp.float32)
    for slot in range(entries.shape[1]):
        accum = accum + (entries[:, slot : slot + 1] == columns[None, :]).astype(jnp.float32)
    return accum.astype(jnp.bfloat16)


def select_rows(values, positions):
    live = (positions >= 0)[..., None]
    picked = values[jnp.maximum(positions, 0)]
    return jnp.where(live, picked, jnp.zeros_like(picked))


def project_back(delta, weight):
    return lax.dot_general(
        delta, weight, (((1,), (1,)), ((), ())), preferred_element_type=jnp.float32
    )


def contract_rows(left_side, right_side):
    return lax.dot_general(
        left_side, right_side, (((0,), (0,)), ((), ())), preferred_element_type=jnp.float32
    )


def silu_slope(value):
    sigma = jax.nn.sigmoid(value)
    return sigma * (1.0 + value * (1.0 - sigma))


def edge_rows(from_authors, from_papers):
    stacked = jnp.stack([from_authors, from_papers])
    width = stacked.shape[-1]
    arrived = lax.all_to_all(stacked, ("row", "col"), split_axis=1, concat_axis=1, tiled=True)
    return (arrived[0].reshape(-1, width), arrived[1].reshape(-1, width))


def per_device(
    x_paper,
    x_author,
    cite_nbr,
    write_src,
    write_dst,
    w_self_paper,
    w_cite,
    w_write,
    w_self_author,
    w_written,
    grad_paper,
    grad_author,
):
    papers = x_paper.shape[0]
    authors = x_author.shape[0]
    cnt_cite = jnp.maximum(jnp.sum((cite_nbr >= 0).astype(jnp.float32), axis=1, keepdims=True), 1.0)
    rows_in = lax.all_gather(x_paper, "col", axis=0, tiled=True)
    columns = lax.iota(jnp.int32, rows_in.shape[0])
    cite_total = jnp.dot(
        match_table(cite_nbr, columns), rows_in, preferred_element_type=jnp.float32
    )
    cited = (cite_total / cnt_cite).astype(jnp.bfloat16)
    send_list = write_src[0]
    take_list = write_dst[0]
    table_paper = (take_list.reshape(-1)[None, :] == lax.iota(jnp.int32, papers)[:, None]).astype(
        jnp.bfloat16
    )
    table_author = (send_list.reshape(-1)[None, :] == lax.iota(jnp.int32, authors)[:, None]).astype(
        jnp.bfloat16
    )
    cnt_write = jnp.maximum(jnp.sum(table_paper, axis=1, keepdims=True, dtype=jnp.float32), 1.0)
    cnt_written = jnp.maximum(jnp.sum(table_author, axis=1, keepdims=True, dtype=jnp.float32), 1.0)
    into_papers, into_authors = edge_rows(
        select_rows(x_author, send_list), select_rows(x_paper, take_list)
    )
    written = (
        jnp.dot(table_paper, into_papers, preferred_element_type=jnp.float32) / cnt_write
    ).astype(jnp.bfloat16)
    authored = (
        jnp.dot(table_author, into_authors, preferred_element_type=jnp.float32) / cnt_written
    ).astype(jnp.bfloat16)
    pre_paper = (
        jnp.dot(x_paper, w_self_paper, preferred_element_type=jnp.float32)
        + jnp.dot(cited, w_cite, preferred_element_type=jnp.float32)
        + jnp.dot(written, w_write, preferred_element_type=jnp.float32)
    )
    pre_author = jnp.dot(x_author, w_self_author, preferred_element_type=jnp.float32) + jnp.dot(
        authored, w_written, preferred_element_type=jnp.float32
    )
    out_paper = jax.nn.silu(pre_paper).astype(jnp.bfloat16)
    out_author = jax.nn.silu(pre_author).astype(jnp.bfloat16)
    dpre_paper = (grad_paper.astype(jnp.float32) * silu_slope(pre_paper)).astype(jnp.bfloat16)
    dpre_author = (grad_author.astype(jnp.float32) * silu_slope(pre_author)).astype(jnp.bfloat16)
    dz_cite = (project_back(dpre_paper, w_cite) / cnt_cite).astype(jnp.bfloat16)
    dz_write = (project_back(dpre_paper, w_write) / cnt_write).astype(jnp.bfloat16)
    dz_written = (project_back(dpre_author, w_written) / cnt_written).astype(jnp.bfloat16)
    columns = lax.iota(jnp.int32, lax.axis_size("col") * papers)
    cite_grad = lax.psum_scatter(
        contract_rows(match_table(cite_nbr, columns), dz_cite),
        "col",
        scatter_dimension=0,
        tiled=True,
    )
    back_papers, back_authors = edge_rows(
        select_rows(dz_written, send_list), select_rows(dz_write, take_list)
    )
    dx_paper = (
        project_back(dpre_paper, w_self_paper)
        + cite_grad
        + jnp.dot(table_paper, back_papers, preferred_element_type=jnp.float32)
    ).astype(jnp.bfloat16)
    dx_author = (
        project_back(dpre_author, w_self_author)
        + jnp.dot(table_author, back_authors, preferred_element_type=jnp.float32)
    ).astype(jnp.bfloat16)
    local_grads = jnp.stack(
        [
            contract_rows(x_paper, dpre_paper),
            contract_rows(cited, dpre_paper),
            contract_rows(written, dpre_paper),
            contract_rows(x_author, dpre_author),
            contract_rows(authored, dpre_author),
        ]
    )
    halfway = lax.psum_scatter(local_grads, "row", scatter_dimension=1, tiled=True)
    summed = lax.psum_scatter(halfway, "col", scatter_dimension=2, tiled=True)
    devices_all = lax.axis_size("row") * lax.axis_size("col")
    paper_scale = float(papers * devices_all) ** (-0.5)
    author_scale = float(authors * devices_all) ** (-0.5)
    factors = jnp.array(
        [paper_scale, paper_scale, paper_scale, author_scale, author_scale], jnp.float32
    )
    dweights = summed * factors[:, None, None]
    return (out_paper, out_author, dx_paper, dx_author, dweights)


def solution(mesh):
    placed = (
        P(("row", "col"), None),
        P(("row", "col"), None),
        P(("row", "col"), None),
        P(("row", "col"), None, None),
        P(("row", "col"), None, None),
        P(),
        P(),
        P(),
        P(),
        P(),
        P(("row", "col"), None),
        P(("row", "col"), None),
    )
    return jax.shard_map(
        per_device,
        mesh=mesh,
        in_specs=placed,
        out_specs=(
            P(("row", "col"), None),
            P(("row", "col"), None),
            P(("row", "col"), None),
            P(("row", "col"), None),
            P(None, "row", "col"),
        ),
        check_vma=False,
    )
```

profile of v0, /device:TPU:0, one launch (start us, length us, event | category | flops | bytes accessed | tf_op | source)
XLA Modules:
  0.0 510.0 jit_solution(10885800553670908441)
XLA Ops:
  11.3 2.0 gather_fusion.1
  15.7 7.3 %all-to-all-start = ((bf16[2,32,4,768]{3,2,0,1:T(4,128)(2,1)}), bf16[2,32,4,768]{3,2,0,1:T(4,128)(2,1)S(1)}, u32[]{:S(2)}, u32[]{:S(2)}) async-start(bf16[2,32,4,768]{3,2,0,1:T(4,128)(2,1)} %pad_maximum_fusion), calls=%async_computation | async-start | bytes 786432 | tf_op jit(solution)/shard_map/all_to_all | solution.py:40
  23.8 3.1 fusion.19
  26.9 1.6 fusion.20
  28.5 18.3 %all-to-all-done = bf16[2,32,4,768]{3,2,0,1:T(4,128)(2,1)S(1)} async-done(((bf16[2,32,4,768]{3,2,0,1:T(4,128)(2,1)}), bf16[2,32,4,768]{3,2,0,1:T(4,128)(2,1)S(1)}, u32[]{:S(2)}, u32[]{:S(2)}) %all-to-all-start) | async-done | bytes 393248 | tf_op jit(solution)/shard_map/all_to_all | solution.py:40
  49.3 1.7 multiply_convert_fusion
  51.1 30.5 %all-gather.2.cloned.1.call-done = bf16[2048,768]{1,0:T(8,128)(2,1)} async-done(((bf16[256,768]{1,0:T(8,128)(2,1)}), bf16[2048,768]{1,0:T(8,128)(2,1)}) %all-gather.2.cloned.1.call-update) | async-done | bytes 3145744 | tf_op jit(solution)/shard_map/all_gather | solution.py:61
  81.6 6.9 %fusion.7 = bf16[256,768]{1,0:T(8,128)(2,1)S(1)} fusion(bf16[2048,768]{1,0:T(8,128)(2,1)} %all-gather.2.cloned.1.call-done, f32[256]{0:T(256)S(1)} %broadcast_maximum_fusion.4, s32[256]{0:T(256)S(1)} %bitcast.123, s32[256]{0:T(256)S(1)} %bitcast.95, s32[256]{0:T(256)S(1)} %bitcast.97, s32[256]{0:T(256)S(1)} %bitcast.99, s32[256]{0:T(256)S(1)} %bitcast.101, ...), kind=kOutput, calls=%fused_computation.45 | convolution fusion | flops 830865408 | bytes 3556352 | tf_op jit(solution)/shard_map/dot_general | solution.py:63
  90.1 1.7 multiply_convert_fusion.1
  91.8 2.3 bitcast_dynamic-update-slice_fusion.1
  94.1 2.4 bitcast_dynamic-update-slice_fusion.4
  96.5 2.2 bitcast_dynamic-update-slice_fusion.3
  98.8 2.3 bitcast_dynamic-update-slice_fusion
  101.1 2.2 bitcast_dynamic-update-slice_fusion.2
  103.4 21.0 %copy.69 = f32[5,768,1024]{2,0,1:T(8,128)} copy(f32[5,768,1024]{1,2,0:T(8,128)} %bitcast_dynamic-update-slice_fusion.2) | data formatting | bytes 31457280
  124.4 21.5 %copy.71 = f32[96,8,5,1024]{3,1,2,0:T(8,128)} copy(f32[96,8,5,1024]{3,2,1,0:T(8,128)} %bitcast.90) | data formatting | bytes 31457280
  146.0 8.5 %fusion.8 = f32[2048,768]{1,0:T(8,128)} fusion(bf16[256,1024]{1,0:T(8,128)(2,1)S(1)} %get-tuple-element.27, bf16[768,1024]{1,0:T(8,128)(2,1)S(1)} %copy-done, f32[256]{0:T(256)S(1)} %broadcast_maximum_fusion.4, s32[256]{0:T(256)S(1)} %bitcast.124, s32[256]{0:T(256)S(1)} %bitcast.96, s32[256]{0:T(256)S(1)} %bitcast.98, s32[256]{0:T(256)S(1)} %bitcast.100, ...), kind=kOutput, calls=%fused_computation.46 | convolution fusion | flops 1233518592 | bytes 8406016 | tf_op jit(solution)/shard_map/dot_general | solution.py:27
  154.6 110.0 %reduce-scatter.10.cloned.1.call-done = f32[192,5120]{1,0:T(8,128)} async-done(((f32[768,5120]{1,0:T(8,128)}), f32[192,5120]{1,0:T(8,128)}) %reduce-scatter.10.cloned.1.call-update) | async-done | bytes 3932176
  264.6 6.8 %reshape.136 = f32[192,5,1024]{2,1,0:T(8,128)} reshape(f32[192,5120]{1,0:T(8,128)} %reduce-scatter.10.cloned.1.call-done) | data formatting | bytes 7864320
  271.3 6.8 %copy.70 = f32[5,192,1024]{1,2,0:T(8,128)} copy(f32[5,192,1024]{2,0,1:T(8,128)} %bitcast.92) | data formatting | bytes 7864320
  278.1 2.0 fusion.3
  281.9 2.0 fusion.4
  285.1 1.9 pad_maximum_fusion.1
  287.0 4.7 all-to-all-start.1
  291.7 2.1 fusion.21
  293.8 22.5 %all-to-all-done.1 = bf16[2,32,4,768]{3,2,0,1:T(4,128)(2,1)} async-done(((bf16[2,32,4,768]{3,2,0,1:T(4,128)(2,1)}), bf16[2,32,4,768]{3,2,0,1:T(4,128)(2,1)}, u32[]{:S(2)}, u32[]{:S(2)}) %all-to-all-start.1) | async-done | bytes 393248 | tf_op jit(solution)/shard_map/all_to_all | solution.py:40
  316.3 1.2 fusion.16
  318.6 77.1 %reduce-scatter.6.cloned.1.call-done = f32[256,768]{1,0:T(8,128)} async-done(((f32[2048,768]{1,0:T(8,128)}), f32[256,768]{1,0:T(8,128)}) %reduce-scatter.6.cloned.1.call-update) | async-done | bytes 786448 | tf_op jit(solution)/shard_map/reduce_scatter | solution.py:102
  395.7 2.2 convolution_add_fusion.5
  398.9 102.4 %reduce-scatter.8.cloned.1.call-done = f32[5,192,128]{1,2,0:T(8,128)} async-done(((f32[5,192,1024]{1,2,0:T(8,128)}), f32[5,192,128]{1,2,0:T(8,128)}) %reduce-scatter.8.cloned.1.call-update) | async-done | bytes 491536 | tf_op jit(solution)/shard_map/reduce_scatter | solution.py:130
  501.3 1.1 broadcast_multiply_fusion
  502.4 1.0 copy.65
  (84 shorter events, 16.4 us)
Async XLA Ops:
  7.2 81.3 %copy-start = (bf16[768,1024]{1,0:T(8,128)(2,1)S(1)}, bf16[768,1024]{1,0:T(8,128)(2,1)}, u32[]{:S(2)}) copy-start(bf16[768,1024]{1,0:T(8,128)(2,1)} %param.19) | copy-start | bytes 4718596
  7.2 6.2 %copy-start.2 = (bf16[256,768]{1,0:T(8,128)(2,1)S(1)}, bf16[256,768]{1,0:T(8,128)(2,1)}, u32[]{:S(2)}) copy-start(bf16[256,768]{1,0:T(8,128)(2,1)} %param.14) | copy-start | bytes 1179652
  7.2 74.4 %all-gather.2.cloned.1.call-start = ((), (), s32[]{:S(2)}) async-start(), calls=%async_computation.5 | async-start | bytes 3538944 | tf_op jit(solution)/shard_map/all_gather | solution.py:61
  13.4 9.7 %copy-start.10 = (s32[1,32,4]{1,2,0:T(4,128)S(1)}, s32[1,32,4]{1,2,0:T(4,128)}, u32[]{:S(2)}) copy-start(s32[1,32,4]{1,2,0:T(4,128)} %param.16) | copy-start | bytes 1540
  13.4 9.8 %copy-start.11 = (s32[1,32,4]{1,2,0:T(4,128)S(1)}, s32[1,32,4]{1,2,0:T(4,128)}, u32[]{:S(2)}) copy-start(s32[1,32,4]{1,2,0:T(4,128)} %param.17) | copy-start | bytes 1540
  13.4 10.0 %copy-start.9 = (s32[256,16]{0,1:T(8,128)S(1)}, s32[256,16]{0,1:T(8,128)}, u32[]{:S(2)}) copy-start(s32[256,16]{0,1:T(8,128)} %param.15) | copy-start | bytes 49156
  13.4 10.4 %copy-start.1 = (bf16[256,768]{1,0:T(8,128)(2,1)S(1)}, bf16[256,768]{1,0:T(8,128)(2,1)}, u32[]{:S(2)}) copy-start(bf16[256,768]{1,0:T(8,128)(2,1)} %param.13) | copy-start | bytes 1179652
  15.7 31.0 %all-to-all-start = ((bf16[2,32,4,768]{3,2,0,1:T(4,128)(2,1)}), bf16[2,32,4,768]{3,2,0,1:T(4,128)(2,1)S(1)}, u32[]{:S(2)}, u32[]{:S(2)}) async-start(bf16[2,32,4,768]{3,2,0,1:T(4,128)(2,1)} %pad_maximum_fusion), calls=%async_computation | async-start | bytes 786432 | tf_op jit(solution)/shard_map/all_to_all | solution.py:40
  23.0 241.6 %reduce-scatter.10.cloned.1.call-start = ((), (), s32[]{:S(2)}) async-start(), calls=%async_computation.8 | async-start | bytes 19660800
  23.5 3.5 copy-start.3
  47.0 1.3 copy-start.14
  47.3 3.8 copy-start.6
  47.3 1.5 copy-start.5
  47.3 2.0 copy-start.12
  81.6 6.9 %copy-start.4 = (f32[256,1024]{1,0:T(8,128)S(1)}, f32[256,1024]{1,0:T(8,128)}, u32[]{:S(2)}) copy-start(f32[256,1024]{1,0:T(8,128)} %fusion.19) | copy-start | bytes 3145732
  88.4 1.0 copy-start.8
  88.5 1.5 copy-start.13
  88.5 1.6 copy-start.15
  98.8 2.4 copy-start.7
  145.9 249.7 %reduce-scatter.6.cloned.1.call-start = ((), (), s32[]{:S(2)}) async-start(), calls=%async_computation.6 | async-start | bytes 7077888 | tf_op jit(solution)/shard_map/reduce_scatter | solution.py:102
  154.5 346.8 %reduce-scatter.8.cloned.1.call-start = ((), (), s32[]{:S(2)}) async-start(), calls=%async_computation.7 | async-start | bytes 5898240 | tf_op jit(solution)/shard_map/reduce_scatter | solution.py:130
  287.0 29.3 %all-to-all-start.1 = ((bf16[2,32,4,768]{3,2,0,1:T(4,128)(2,1)}), bf16[2,32,4,768]{3,2,0,1:T(4,128)(2,1)}, u32[]{:S(2)}, u32[]{:S(2)}) async-start(bf16[2,32,4,768]{3,2,0,1:T(4,128)(2,1)} %pad_maximum_fusion.1), calls=%async_computation.2 | async-start | bytes 786432 | tf_op jit(solution)/shard_map/all_to_all | solution.py:40
Sparse Core Ops, SparseCore 0:
  10.2 71.2 all-gather.1
  146.1 118.4 reduce-scatter.9
  268.2 127.4 reduce-scatter.5
  399.1 102.0 reduce-scatter.7
where the time goes:
time: 511 us; the launch traced here: 510 us
  waiting for transfers between devices  362 us (71%)
  local copies, waits for them, and re-layouts  66.5 us (13%)
  matrix products  47.2 us (9%)
  between operations  14.1 us (3%)
  starting transfers between devices  12.1 us (2%)
  other arithmetic  8.42 us (2%)
    unnamed x5, waiting for transfers between devices  111 us
    reduce_scatter x1, waiting for transfers between devices, per_device(): summed = lax.psum_scatter(halfway, 'col', scatter_dimension=2, tiled=True)  102 us
    reduce_scatter x1, waiting for transfers between devices, per_device(): lax.psum_scatter(contract_rows(match_table(cite_nbr, columns), dz_cite),...  77.1 us
    unnamed x39, local copies, waits for them, and re-layouts  59.4 us
    all_to_all x2, waiting for transfers between devices, edge_rows(): lax.all_to_all(stacked, ('row', 'col'), split_axis=1, concat_axis=1, tile...  40.8 us
    all_gather x1, waiting for transfers between devices, per_device(): rows_in = lax.all_gather(x_paper, 'col', axis=0, tiled=True)  30.5 us
    dot_general x6, matrix products, contract_rows(): lax.dot_general(left_side, right_side, (((0,), (0,)), ((), ())), preferre...  20 us
    all_to_all x2, starting transfers between devices, edge_rows(): lax.all_to_all(stacked, ('row', 'col'), split_axis=1, concat_axis=1, tile...  12 us
  transfers between devices with their start and end apart: 6, of which 6 were waited for; matrix products, arithmetic and copies ran while one was open for 11% of the time, Pallas kernels for 0%

commit v1 on v0

--- a/solution.py
+++ b/solution.py
@@ -39,6 +39,94 @@
     width = stacked.shape[-1]
     arrived = lax.all_to_all(stacked, ("row", "col"), split_axis=1, concat_axis=1, tiled=True)
     return (arrived[0].reshape(-1, width), arrived[1].reshape(-1, width))
+
+
+def pick_half(value, low, high):
+    return jnp.where(value == 0, low, high)
+
+
+def neighbour_blocks(block):
+    size = lax.axis_size("col")
+    me = lax.axis_index("col")
+    if size % 2:
+        sources = lax.rem(me + lax.iota(jnp.int32, size), size)
+        rows = lax.all_gather(block, "col", axis=0)
+        return rows[sources].reshape(-1, block.shape[1]), sources
+    depth = size // 2
+    level = me // 2
+
+    def across(value, valid):
+        return lax.ppermute(value, "col", [(c, c ^ 1) for c in range(size) if valid(c // 2)])
+
+    ups, downs = [block], [block]
+    for hop in range(1, depth):
+        ups.append(
+            lax.ppermute(
+                ups[-1], "col", [(c, c + 2) for c in range(size - 2) if c // 2 >= hop - 1]
+            )
+        )
+        downs.append(
+            lax.ppermute(
+                downs[-1], "col", [(c, c - 2) for c in range(2, size) if c // 2 <= depth - hop]
+            )
+        )
+    parts = [block, across(block, lambda z: True)]
+    sources = [me, me ^ 1]
+    ups_across = [None] + [
+        across(ups[hop], lambda z, hop=hop: z >= hop) for hop in range(1, depth)
+    ]
+    downs_across = [None] + [
+        across(downs[hop], lambda z, hop=hop: z < depth - hop) for hop in range(1, depth)
+    ]
+    for hop in range(1, depth):
+        source = lax.rem(level - hop + depth, depth) * 2 + me % 2
+        parts.append(jnp.where(level >= hop, ups[hop], downs[depth - hop]))
+        parts.append(jnp.where(level >= hop, ups_across[hop], downs_across[depth - hop]))
+        sources += [source, source ^ 1]
+    return jnp.concatenate(parts, axis=0), jnp.stack(sources)
+
+
+def swap(value, axis, bit):
+    size = lax.axis_size(axis)
+    return lax.ppermute(value, axis, [(i, i ^ bit) for i in range(size)])
+
+
+def block_order(size):
+    bits = size.bit_length() - 1
+    return [sum(((i >> b) & 1) << (bits - 1 - b) for b in range(bits)) for i in range(size)]
+
+
+def columns_by_lowest_bit(values):
+    size = lax.axis_size("col")
+    width = values.shape[1] // size
+    return jnp.concatenate(
+        [values[:, i * width : (i + 1) * width] for i in block_order(size)], axis=1
+    )
+
+
+def scatter_sum(partial, matrices):
+    rows = lax.axis_size("row")
+    value = partial.reshape(matrices, rows, -1, partial.shape[1])
+    me = lax.axis_index("row")
+    bit = 1
+    while bit < rows:
+        mine = (me // bit) % 2
+        split = value.reshape(matrices, value.shape[1] // 2, 2, value.shape[2], value.shape[3])
+        keep = lax.dynamic_index_in_dim(split, mine, 2, keepdims=False)
+        send = lax.dynamic_index_in_dim(split, 1 - mine, 2, keepdims=False)
+        value = keep + swap(send.astype(jnp.bfloat16), "row", bit).astype(jnp.float32)
+        bit *= 2
+    value = value.reshape(-1, value.shape[3])
+    me = lax.axis_index("col")
+    bit = 1
+    while bit < lax.axis_size("col"):
+        mine = (me // bit) % 2
+        half = value.shape[1] // 2
+        low, high = value[:, :half], value[:, half:]
+        send = pick_half(mine, high, low).astype(jnp.bfloat16)
+        value = pick_half(mine, low, high) + swap(send, "col", bit).astype(jnp.float32)
+        bit *= 2
+    return value.reshape(matrices, -1, value.shape[1])
 
 
 def per_device(
@@ -58,11 +146,16 @@
     papers = x_paper.shape[0]
     authors = x_author.shape[0]
     cnt_cite = jnp.maximum(jnp.sum((cite_nbr >= 0).astype(jnp.float32), axis=1, keepdims=True), 1.0)
-    rows_in = lax.all_gather(x_paper, "col", axis=0, tiled=True)
-    columns = lax.iota(jnp.int32, rows_in.shape[0])
-    cite_total = jnp.dot(
-        match_table(cite_nbr, columns), rows_in, preferred_element_type=jnp.float32
-    )
+    rows_in, sources = neighbour_blocks(x_paper)
+    positions = lax.iota(jnp.int32, papers)
+    columns = (sources[:, None] * papers + positions[None, :]).reshape(-1)
+    table_cite = lax.optimization_barrier(match_table(cite_nbr, columns))
+    nbr_all = lax.all_gather(cite_nbr, "col", axis=0)
+    nbr_here = nbr_all[sources].reshape(-1, cite_nbr.shape[1])
+    table_cited = lax.optimization_barrier(
+        match_table(nbr_here, lax.axis_index("col") * papers + positions)
+    )
+    cite_total = jnp.dot(table_cite, rows_in, preferred_element_type=jnp.float32)
     cited = (cite_total / cnt_cite).astype(jnp.bfloat16)
     send_list = write_src[0]
     take_list = write_dst[0]
@@ -98,13 +191,8 @@
     dz_cite = (project_back(dpre_paper, w_cite) / cnt_cite).astype(jnp.bfloat16)
     dz_write = (project_back(dpre_paper, w_write) / cnt_write).astype(jnp.bfloat16)
     dz_written = (project_back(dpre_author, w_written) / cnt_written).astype(jnp.bfloat16)
-    columns = lax.iota(jnp.int32, lax.axis_size("col") * papers)
-    cite_grad = lax.psum_scatter(
-        contract_rows(match_table(cite_nbr, columns), dz_cite),
-        "col",
-        scatter_dimension=0,
-        tiled=True,
-    )
+    dz_rows, _ = neighbour_blocks(dz_cite)
+    cite_grad = contract_rows(table_cited, dz_rows)
     back_papers, back_authors = edge_rows(
         select_rows(dz_written, send_list), select_rows(dz_write, take_list)
     )
@@ -117,17 +205,16 @@
         project_back(dpre_author, w_self_author)
         + jnp.dot(table_author, back_authors, preferred_element_type=jnp.float32)
     ).astype(jnp.bfloat16)
-    local_grads = jnp.stack(
-        [
-            contract_rows(x_paper, dpre_paper),
-            contract_rows(cited, dpre_paper),
-            contract_rows(written, dpre_paper),
-            contract_rows(x_author, dpre_author),
-            contract_rows(authored, dpre_author),
-        ]
-    )
-    halfway = lax.psum_scatter(local_grads, "row", scatter_dimension=1, tiled=True)
-    summed = lax.psum_scatter(halfway, "col", scatter_dimension=2, tiled=True)
+    turned_paper = columns_by_lowest_bit(dpre_paper)
+    turned_author = columns_by_lowest_bit(dpre_author)
+    author_sums = scatter_sum(
+        contract_rows(jnp.concatenate([x_author, authored], axis=1), turned_author), 2
+    )
+    pair_sums = scatter_sum(
+        contract_rows(jnp.concatenate([x_paper, written], axis=1), turned_paper), 2
+    )
+    cited_sum = scatter_sum(contract_rows(cited, turned_paper), 1)
+    summed = jnp.concatenate([pair_sums[:1], cited_sum, pair_sums[1:], author_sums], axis=0)
     devices_all = lax.axis_size("row") * lax.axis_size("col")
     paper_scale = float(papers * devices_all) ** (-0.5)
     author_scale = float(authors * devices_all) ** (-0.5)

time: 511 us -> 265 us (0.52)
  waiting for transfers between devices: 362 us -> 66.7 us
  starting transfers between devices: 12.1 us -> 70.5 us
  local copies, waits for them, and re-layouts: 66.5 us -> 26.1 us
  blocking collectives: 0 us -> 35.4 us
  other arithmetic: 8.42 us -> 35.6 us
  matrix products: 47.2 us -> 27.5 us
  between operations: 14.1 us -> 1.8 us
    reduce_scatter x2 -> x0, waiting for transfers between devices: 179 us -> none  [the longest x1 102 us: per_device(): summed = lax.psum_scatter(halfway, 'col', scatter_dimension=2, tiled=True)]
    unnamed x5 -> x0, waiting for transfers between devices: 111 us -> none
    ppermute x0 -> x41, waiting for transfers between devices: none -> 66.5 us  [the longest x15 29.7 us: swap(): return lax.ppermute(value, axis, [(i, i ^ bit) for i in range(size)])]
    ppermute x0 -> x41, starting transfers between devices: none -> 63.9 us  [the longest x14 25.8 us: across(): lax.ppermute(value, 'col', [(c, c ^ 1) for c in range(size) if valid(c //...]
    unnamed x39 -> x84, local copies, waits for them, and re-layouts: 59.4 us -> 10.7 us
    all_to_all x2, waiting for transfers between devices: 40.8 us -> 0.22 us  [edge_rows(): lax.all_to_all(stacked, ('row', 'col'), split_axis=1, concat_axis=1, tile...]
    all_gather x0 -> x1, blocking collectives: none -> 35.4 us  [per_device(): nbr_all = lax.all_gather(cite_nbr, 'col', axis=0)]
    all_gather x1 -> x0, waiting for transfers between devices: 30.5 us -> none  [per_device(): rows_in = lax.all_gather(x_paper, 'col', axis=0, tiled=True)]
  transfers between devices with their start and end apart: 6 -> 43, of which waited for: 6 -> 16; matrix products, arithmetic and copies ran while one was open for 11% -> 31% of each run, Pallas kernels for 0% -> 0%
where the time goes in v1:
time: 265 us; the launch traced here: 264 us
  starting transfers between devices  70.5 us (27%)
  waiting for transfers between devices  66.7 us (25%)
  other arithmetic  35.6 us (13%)
  blocking collectives  35.4 us (13%)
  matrix products  27.5 us (10%)
  local copies, waits for them, and re-layouts  26.1 us (10%)
    all_gather x1, blocking collectives, per_device(): nbr_all = lax.all_gather(cite_nbr, 'col', axis=0)  35.4 us
    ppermute x15, waiting for transfers between devices, swap(): return lax.ppermute(value, axis, [(i, i ^ bit) for i in range(size)])  29.7 us
    ppermute x14, starting transfers between devices, across(): lax.ppermute(value, 'col', [(c, c ^ 1) for c in range(size) if valid(c //...  25.8 us
    ppermute x14, waiting for transfers between devices, across(): lax.ppermute(value, 'col', [(c, c ^ 1) for c in range(size) if valid(c //...  20.6 us
    ppermute x6, waiting for transfers between devices, neighbour_blocks(): lax.ppermute(downs[-1], 'col', [(c, c - 2) for c in range(2, size) if c /...  16.2 us
    ppermute x15, starting transfers between devices, swap(): return lax.ppermute(value, axis, [(i, i ^ bit) for i in range(size)])  15.2 us
    ppermute x6, starting transfers between devices, neighbour_blocks(): lax.ppermute(ups[-1], 'col', [(c, c + 2) for c in range(size - 2) if c //...  15.1 us
    unnamed x84, local copies, waits for them, and re-layouts  10.7 us
  transfers between devices with their start and end apart: 43, of which 16 were waited for; matrix products, arithmetic and copies ran while one was open for 31% of the time, Pallas kernels for 0%

profile of v1, /device:TPU:0, one launch (start us, length us, event | category | flops | bytes accessed | tf_op | source)
XLA Modules:
  0.0 263.6 jit_solution(5464303657014684410)
XLA Ops:
  2.1 6.3 %collective-permute-start.1 = (bf16[256,768]{1,0:T(8,128)(2,1)}, bf16[256,768]{1,0:T(8,128)(2,1)}, u32[]{:S(2)}, u32[]{:S(2)}) collective-permute-start(bf16[256,768]{1,0:T(8,128)(2,1)} %param.13), channel_id=1, source_target_pairs={{0,2},{1,3},{2,4},{3,5},{4,6},{5,7},{8,10},{9,11},{10,12},{11,13},... | collective-permute-start | bytes 1179656 | tf_op jit(solution)/shard_map/ppermute | solution.py:64
  16.8 4.0 %all-to-all-start = ((bf16[2,32,4,768]{3,2,0,1:T(4,128)(2,1)}), bf16[2,32,4,768]{3,2,0,1:T(4,128)(2,1)S(1)}, u32[]{:S(2)}, u32[]{:S(2)}) async-start(bf16[2,32,4,768]{3,2,0,1:T(4,128)(2,1)} %pad_maximum_fusion), calls=%async_computation | async-start | bytes 786432 | tf_op jit(solution)/shard_map/all_to_all | solution.py:40
  21.1 35.4 %all-gather = s32[2048,16]{0,1:T(8,128)S(1)} all-gather(s32[256,16]{0,1:T(8,128)S(1)} %copy-done.22), channel_id=2, replica_groups=mesh['row'=4,'col'=8] {'col'}, dimensions={0}, use_global_device_ids=true | all-gather | bytes 147456 | tf_op jit(solution)/shard_map/all_gather | solution.py:153
  56.6 4.4 %add_convert_fusion.1 = bf16[256,2048]{1,0:T(8,128)(2,1)} fusion(s32[2048]{0:T(1024)S(1)} %bitcast.174, s32[256]{0:T(256)S(1)} %bitcast.176, s32[256]{0:T(256)S(1)} %bitcast.177, s32[256]{0:T(256)S(1)} %bitcast.178, s32[256]{0:T(256)S(1)} %bitcast.179, s32[256]{0:T(256)S(1)} %bitcast.180, s32[256]{0:T(256)S(1)} %bitcast.181, s32[256]{0:T(256)S(1)} %bitcast.182, ...), kind=kLoop, calls=%fused_computation.10 | loop fusion | flops 25165824 | bytes 1073152 | tf_op jit(solution)/shard_map/convert_element_type | solution.py:11
  61.0 3.0 %fusion.32 = f32[256,1024]{1,0:T(8,128)} fusion(bf16[256,768]{1,0:T(8,128)(2,1)S(1)} %copy-done.4, bf16[768,1024]{1,0:T(8,128)(2,1)} %param.18), kind=kOutput, calls=%fused_computation.148 | convolution fusion | flops 402653184 | bytes 3014656 | tf_op jit(solution)/shard_map/dot_general | solution.py:180
  65.3 5.7 %add_convert_fusion = bf16[2048,256]{1,0:T(8,128)(2,1)} fusion(s32[256]{0:T(256)S(1)} %iota_add_fusion, s32[2048]{0:T(1024)S(1)} %bitcast.159, s32[2048]{0:T(1024)S(1)} %bitcast.160, s32[2048]{0:T(1024)S(1)} %bitcast.161, s32[2048]{0:T(1024)S(1)} %bitcast.162, s32[2048]{0:T(1024)S(1)} %bitcast.163, s32[2048]{0:T(1024)S(1)} %bitcast.164, ...), kind=kLoop, calls=%fused_computation.9 | loop fusion | flops 25165824 | bytes 1180672 | tf_op jit(solution)/shard_map/convert_element_type | solution.py:11
  71.8 3.0 %fusion.33 = f32[256,1024]{1,0:T(8,128)} fusion(bf16[256,768]{1,0:T(8,128)(2,1)S(1)} %copy-done.5, bf16[768,1024]{1,0:T(8,128)(2,1)} %param.21), kind=kOutput, calls=%fused_computation.149 | convolution fusion | flops 402653184 | bytes 3014656 | tf_op jit(solution)/shard_map/dot_general | solution.py:184
  97.1 2.2 fusion.35
  100.0 7.2 %collective-permute-done.4 = bf16[256,768]{1,0:T(8,128)(2,1)} collective-permute-done((bf16[256,768]{1,0:T(8,128)(2,1)}, bf16[256,768]{1,0:T(8,128)(2,1)}, u32[]{:S(2)}, u32[]{:S(2)}) %collective-permute-start.4) | collective-permute-done | bytes 393248 | tf_op jit(solution)/shard_map/ppermute | solution.py:69
  107.1 3.7 %collective-permute-start.6 = (bf16[256,768]{1,0:T(8,128)(2,1)}, bf16[256,768]{1,0:T(8,128)(2,1)S(1)}, u32[]{:S(2)}, u32[]{:S(2)}) collective-permute-start(bf16[256,768]{1,0:T(8,128)(2,1)} %collective-permute-done.4), channel_id=1, source_target_pairs={{0,1},{1,0},{8,9},{9,8},{16,17},{17,16},{24,25},{25,24}} | collective-permute-start | bytes 1179656 | tf_op jit(solution)/shard_map/ppermute | solution.py:59
  115.7 5.5 %collective-permute-done.6 = bf16[256,768]{1,0:T(8,128)(2,1)S(1)} collective-permute-done((bf16[256,768]{1,0:T(8,128)(2,1)}, bf16[256,768]{1,0:T(8,128)(2,1)S(1)}, u32[]{:S(2)}, u32[]{:S(2)}) %collective-permute-start.6) | collective-permute-done | bytes 393248 | tf_op jit(solution)/shard_map/ppermute | solution.py:59
  125.0 2.8 %collective-permute-done.9 = bf16[256,768]{1,0:T(8,128)(2,1)S(1)} collective-permute-done((bf16[256,768]{1,0:T(8,128)(2,1)}, bf16[256,768]{1,0:T(8,128)(2,1)S(1)}, u32[]{:S(2)}, u32[]{:S(2)}) %collective-permute-start.9) | collective-permute-done | bytes 393248 | tf_op jit(solution)/shard_map/ppermute | solution.py:59
  132.4 3.0 %fusion.9 = bf16[256,768]{1,0:T(8,128)(2,1)S(1)} fusion(bf16[256,2048]{1,0:T(8,128)(2,1)S(1)} %copy-done.17, bf16[2048,768]{1,0:T(8,128)(2,1)} %select_dynamic-update-slice_fusion.6, f32[256]{0:T(256)S(1)} %broadcast_maximum_fusion.4), kind=kOutput, calls=%fused_computation.38 | convolution fusion | flops 805699584 | bytes 4588544 | tf_op jit(solution)/shard_map/dot_general | solution.py:158
  143.4 5.3 %collective-permute-start.14 = (bf16[256,768]{1,0:T(8,128)(2,1)}, bf16[256,768]{1,0:T(8,128)(2,1)}, u32[]{:S(2)}, u32[]{:S(2)}) collective-permute-start(bf16[256,768]{1,0:T(8,128)(2,1)} %get-tuple-element.48), channel_id=1, source_target_pairs={{0,2},{1,3},{2,4},{3,5},{4,6},{5,7},{8,10},{9,11},{10,12},{11,13},... | collective-permute-start | bytes 1179656 | tf_op jit(solution)/shard_map/ppermute | solution.py:64
  155.0 2.6 all-to-all-start.1
  158.6 2.8 %copy-done.3 = f32[1536,1024]{1,0:T(8,128)} copy-done((f32[1536,1024]{1,0:T(8,128)}, f32[1536,1024]{1,0:T(8,128)S(1)}, u32[]{:S(2)}) %copy-start.3) | copy-done | bytes 6291480
  173.4 3.1 %bitcast_add_fusion = f32[2,2,192,1024]{3,2,1,0:T(8,128)S(1)} fusion(bf16[2,2,192,1024]{3,2,1,0:T(8,128)(2,1)} %collective-permute-done.36, f32[2,2,2,192,1024]{4,3,2,1,0:T(8,128)} %bitcast.142, s32[]{:T(128)S(6)} %select_n.333), kind=kLoop, calls=%fused_computation.5 | loop fusion | flops 1572864 | bytes 7864324 | tf_op jit(solution)/shard_map/add | solution.py:117
  176.5 4.3 %collective-permute-done.32 = bf16[1,1,192,1024]{3,2,1,0:T(8,128)(2,1)} collective-permute-done((bf16[1,1,192,1024]{3,2,1,0:T(8,128)(2,1)S(1)}, bf16[1,1,192,1024]{3,2,1,0:T(8,128)(2,1)}, u32[]{:S(2)}, u32[]{:S(2)}) %collective-permute-start.32) | collective-permute-done | bytes 393248 | tf_op jit(solution)/shard_map/ppermute | solution.py:91
  184.6 3.6 %collective-permute-done.33 = bf16[192,512]{1,0:T(8,128)(2,1)S(1)} collective-permute-done((bf16[192,512]{1,0:T(8,128)(2,1)S(1)}, bf16[192,512]{1,0:T(8,128)(2,1)S(1)}, u32[]{:S(2)}, u32[]{:S(2)}) %collective-permute-start.33) | collective-permute-done | bytes 196640 | tf_op jit(solution)/shard_map/ppermute | solution.py:91
  188.3 3.2 %collective-permute-start.34 = (bf16[192,256]{1,0:T(8,128)(2,1)S(1)}, bf16[192,256]{1,0:T(8,128)(2,1)S(1)}, u32[]{:S(2)}, u32[]{:S(2)}) collective-permute-start(bf16[192,256]{1,0:T(8,128)(2,1)S(1)} %select_convert_fusion.6), channel_id=1, source_target_pairs={{0,2},{1,3},{2,0},{3,1},{4,6},{5,7},{6,4},{7,5},{8,10},{9,11},{10,... | collective-permute-start | bytes 294920 | tf_op jit(solution)/shard_map/ppermute | solution.py:91
  195.5 9.0 %collective-permute-done.17 = bf16[256,768]{1,0:T(8,128)(2,1)S(1)} collective-permute-done((bf16[256,768]{1,0:T(8,128)(2,1)S(1)}, bf16[256,768]{1,0:T(8,128)(2,1)S(1)}, u32[]{:S(2)}, u32[]{:S(2)}) %collective-permute-start.17) | collective-permute-done | bytes 393248 | tf_op jit(solution)/shard_map/ppermute | solution.py:69
  204.6 2.6 collective-permute-start.25
  207.2 2.3 collective-permute-done.35
  210.2 2.6 collective-permute-start.19
  216.0 3.3 %collective-permute-start.22 = (bf16[256,768]{1,0:T(8,128)(2,1)S(1)}, bf16[256,768]{1,0:T(8,128)(2,1)S(1)}, u32[]{:S(2)}, u32[]{:S(2)}) collective-permute-start(bf16[256,768]{1,0:T(8,128)(2,1)S(1)} %collective-permute-done.16), channel_id=1, source_target_pairs={{0,1},{1,0},{2,3},{3,2},{8,9},{9,8},{10,11},{11,10},{16,17},{17,16... | collective-permute-start | bytes 1179656 | tf_op jit(solution)/shard_map/ppermute | solution.py:59
  220.2 6.5 %collective-permute-done.19 = bf16[256,768]{1,0:T(8,128)(2,1)S(1)} collective-permute-done((bf16[256,768]{1,0:T(8,128)(2,1)S(1)}, bf16[256,768]{1,0:T(8,128)(2,1)S(1)}, u32[]{:S(2)}, u32[]{:S(2)}) %collective-permute-start.19) | collective-permute-done | bytes 393248 | tf_op jit(solution)/shard_map/ppermute | solution.py:59
  229.3 5.8 %collective-permute-done.22 = bf16[256,768]{1,0:T(8,128)(2,1)S(1)} collective-permute-done((bf16[256,768]{1,0:T(8,128)(2,1)S(1)}, bf16[256,768]{1,0:T(8,128)(2,1)S(1)}, u32[]{:S(2)}, u32[]{:S(2)}) %collective-permute-start.22) | collective-permute-done | bytes 393248 | tf_op jit(solution)/shard_map/ppermute | solution.py:59
  237.5 2.5 collective-permute-done.38
  242.6 3.4 %collective-permute-done.39 = bf16[384,256]{1,0:T(8,128)(2,1)S(1)} collective-permute-done((bf16[384,256]{1,0:T(8,128)(2,1)S(1)}, bf16[384,256]{1,0:T(8,128)(2,1)S(1)}, u32[]{:S(2)}, u32[]{:S(2)}) %collective-permute-start.39) | collective-permute-done | bytes 196640 | tf_op jit(solution)/shard_map/ppermute | solution.py:91
  246.1 2.5 collective-permute-done.28
  251.5 5.1 %collective-permute-done.29 = bf16[384,256]{1,0:T(8,128)(2,1)S(1)} collective-permute-done((bf16[384,256]{1,0:T(8,128)(2,1)S(1)}, bf16[384,256]{1,0:T(8,128)(2,1)S(1)}, u32[]{:S(2)}, u32[]{:S(2)}) %collective-permute-start.29) | collective-permute-done | bytes 196640 | tf_op jit(solution)/shard_map/ppermute | solution.py:91
  257.7 5.0 %collective-permute-done.30 = bf16[384,128]{1,0:T(8,128)(2,1)S(1)} collective-permute-done((bf16[384,128]{1,0:T(8,128)(2,1)S(1)}, bf16[384,128]{1,0:T(8,128)(2,1)S(1)}, u32[]{:S(2)}, u32[]{:S(2)}) %collective-permute-start.30) | collective-permute-done | bytes 98336 | tf_op jit(solution)/shard_map/ppermute | solution.py:91
  (257 shorter events, 100.2 us)
Async XLA Ops:
  0.7 77.1 %collective-permute-start.2 = (bf16[256,768]{1,0:T(8,128)(2,1)}, bf16[256,768]{1,0:T(8,128)(2,1)}, u32[]{:S(2)}, u32[]{:S(2)}) collective-permute-start(bf16[256,768]{1,0:T(8,128)(2,1)} %param.13), channel_id=1, source_target_pairs={{2,0},{3,1},{4,2},{5,3},{6,4},{7,5},{10,8},{11,9},{12,10},{13,11},... | collective-permute-start | bytes 1179656 | tf_op jit(solution)/shard_map/ppermute | solution.py:69
  2.1 72.8 %collective-permute-start.1 = (bf16[256,768]{1,0:T(8,128)(2,1)}, bf16[256,768]{1,0:T(8,128)(2,1)}, u32[]{:S(2)}, u32[]{:S(2)}) collective-permute-start(bf16[256,768]{1,0:T(8,128)(2,1)} %param.13), channel_id=1, source_target_pairs={{0,2},{1,3},{2,4},{3,5},{4,6},{5,7},{8,10},{9,11},{10,12},{11,13},... | collective-permute-start | bytes 1179656 | tf_op jit(solution)/shard_map/ppermute | solution.py:64
  8.4 72.5 %collective-permute-start = (bf16[256,768]{1,0:T(8,128)(2,1)}, bf16[256,768]{1,0:T(8,128)(2,1)S(1)}, u32[]{:S(2)}, u32[]{:S(2)}) collective-permute-start(bf16[256,768]{1,0:T(8,128)(2,1)} %param.13), channel_id=1, source_target_pairs={{0,1},{1,0},{2,3},{3,2},{4,5},{5,4},{6,7},{7,6},{8,9},{9,8},{10,11... | collective-permute-start | bytes 1179656 | tf_op jit(solution)/shard_map/ppermute | solution.py:59
  16.8 65.0 %all-to-all-start = ((bf16[2,32,4,768]{3,2,0,1:T(4,128)(2,1)}), bf16[2,32,4,768]{3,2,0,1:T(4,128)(2,1)S(1)}, u32[]{:S(2)}, u32[]{:S(2)}) async-start(bf16[2,32,4,768]{3,2,0,1:T(4,128)(2,1)} %pad_maximum_fusion), calls=%async_computation | async-start | bytes 786432 | tf_op jit(solution)/shard_map/all_to_all | solution.py:40
  74.9 38.1 %collective-permute-start.5 = (bf16[256,768]{1,0:T(8,128)(2,1)}, bf16[256,768]{1,0:T(8,128)(2,1)}, u32[]{:S(2)}, u32[]{:S(2)}) collective-permute-start(bf16[256,768]{1,0:T(8,128)(2,1)} %collective-permute-done.1), channel_id=1, source_target_pairs={{2,3},{3,2},{4,5},{5,4},{6,7},{7,6},{10,11},{11,10},{12,13},{13,12... | collective-permute-start | bytes 1179656 | tf_op jit(solution)/shard_map/ppermute | solution.py:59
  76.3 22.9 %collective-permute-start.7 = (bf16[256,768]{1,0:T(8,128)(2,1)}, bf16[256,768]{1,0:T(8,128)(2,1)}, u32[]{:S(2)}, u32[]{:S(2)}) collective-permute-start(bf16[256,768]{1,0:T(8,128)(2,1)} %collective-permute-done.1), channel_id=1, source_target_pairs={{2,4},{3,5},{4,6},{5,7},{10,12},{11,13},{12,14},{13,15},{18,20},{1... | collective-permute-start | bytes 1179656 | tf_op jit(solution)/shard_map/ppermute | solution.py:64
  77.7 16.1 %collective-permute-start.3 = (bf16[256,768]{1,0:T(8,128)(2,1)}, bf16[256,768]{1,0:T(8,128)(2,1)}, u32[]{:S(2)}, u32[]{:S(2)}) collective-permute-start(bf16[256,768]{1,0:T(8,128)(2,1)} %collective-permute-done.2), channel_id=1, source_target_pairs={{2,0},{3,1},{4,2},{5,3},{10,8},{11,9},{12,10},{13,11},{18,16},{19,... | collective-permute-start | bytes 1179656 | tf_op jit(solution)/shard_map/ppermute | solution.py:69
  79.0 51.5 %collective-permute-start.12 = (bf16[256,768]{1,0:T(8,128)(2,1)}, bf16[256,768]{1,0:T(8,128)(2,1)}, u32[]{:S(2)}, u32[]{:S(2)}) collective-permute-start(bf16[256,768]{1,0:T(8,128)(2,1)} %collective-permute-done.2), channel_id=1, source_target_pairs={{0,1},{1,0},{2,3},{3,2},{4,5},{5,4},{8,9},{9,8},{10,11},{11,10},{1... | collective-permute-start | bytes 1179656 | tf_op jit(solution)/shard_map/ppermute | solution.py:59
  92.3 79.8 %collective-permute-start.36 = (bf16[2,2,192,1024]{3,2,1,0:T(8,128)(2,1)}, bf16[2,2,192,1024]{3,2,1,0:T(8,128)(2,1)}, u32[]{:S(2)}, u32[]{:S(2)}) collective-permute-start(bf16[2,2,192,1024]{3,2,1,0:T(8,128)(2,1)} %fusion.1), channel_id=1, source_target_pairs={{0,8},{8,0},{16,24},{24,16},{1,9},{9,1},{17,25},{25,17},{2,10},{10... | collective-permute-start | bytes 4718600 | tf_op jit(solution)/shard_map/ppermute | solution.py:91
  93.8 13.3 %collective-permute-start.4 = (bf16[256,768]{1,0:T(8,128)(2,1)}, bf16[256,768]{1,0:T(8,128)(2,1)}, u32[]{:S(2)}, u32[]{:S(2)}) collective-permute-start(bf16[256,768]{1,0:T(8,128)(2,1)} %collective-permute-done.3), channel_id=1, source_target_pairs={{2,0},{3,1},{10,8},{11,9},{18,16},{19,17},{26,24},{27,25}} | collective-permute-start | bytes 1179656 | tf_op jit(solution)/shard_map/ppermute | solution.py:69
  99.3 14.4 %collective-permute-start.10 = (bf16[256,768]{1,0:T(8,128)(2,1)}, bf16[256,768]{1,0:T(8,128)(2,1)S(1)}, u32[]{:S(2)}, u32[]{:S(2)}) collective-permute-start(bf16[256,768]{1,0:T(8,128)(2,1)} %collective-permute-done.7), channel_id=1, source_target_pairs={{4,6},{5,7},{12,14},{13,15},{20,22},{21,23},{28,30},{29,31}} | collective-permute-start | bytes 1179656 | tf_op jit(solution)/shard_map/ppermute | solution.py:64
  107.1 14.1 %collective-permute-start.6 = (bf16[256,768]{1,0:T(8,128)(2,1)}, bf16[256,768]{1,0:T(8,128)(2,1)S(1)}, u32[]{:S(2)}, u32[]{:S(2)}) collective-permute-start(bf16[256,768]{1,0:T(8,128)(2,1)} %collective-permute-done.4), channel_id=1, source_target_pairs={{0,1},{1,0},{8,9},{9,8},{16,17},{17,16},{24,25},{25,24}} | collective-permute-start | bytes 1179656 | tf_op jit(solution)/shard_map/ppermute | solution.py:59
  112.9 12.0 %collective-permute-start.8 = (bf16[256,768]{1,0:T(8,128)(2,1)}, bf16[256,768]{1,0:T(8,128)(2,1)S(1)}, u32[]{:S(2)}, u32[]{:S(2)}) collective-permute-start(bf16[256,768]{1,0:T(8,128)(2,1)} %collective-permute-done.7), channel_id=1, source_target_pairs={{4,5},{5,4},{6,7},{7,6},{12,13},{13,12},{14,15},{15,14},{20,21},{2... | collective-permute-start | bytes 1179656 | tf_op jit(solution)/shard_map/ppermute | solution.py:59
  113.6 14.2 %collective-permute-start.9 = (bf16[256,768]{1,0:T(8,128)(2,1)}, bf16[256,768]{1,0:T(8,128)(2,1)S(1)}, u32[]{:S(2)}, u32[]{:S(2)}) collective-permute-start(bf16[256,768]{1,0:T(8,128)(2,1)} %collective-permute-done.3), channel_id=1, source_target_pairs={{0,1},{1,0},{2,3},{3,2},{8,9},{9,8},{10,11},{11,10},{16,17},{17,16... | collective-permute-start | bytes 1179656 | tf_op jit(solution)/shard_map/ppermute | solution.py:59
  140.4 24.0 %collective-permute-start.13 = (bf16[256,768]{1,0:T(8,128)(2,1)}, bf16[256,768]{1,0:T(8,128)(2,1)}, u32[]{:S(2)}, u32[]{:S(2)}) collective-permute-start(bf16[256,768]{1,0:T(8,128)(2,1)} %get-tuple-element.48), channel_id=1, source_target_pairs={{0,1},{1,0},{2,3},{3,2},{4,5},{5,4},{6,7},{7,6},{8,9},{9,8},{10,11... | collective-permute-start | bytes 1179656 | tf_op jit(solution)/shard_map/ppermute | solution.py:59
  142.1 29.3 %collective-permute-start.15 = (bf16[256,768]{1,0:T(8,128)(2,1)}, bf16[256,768]{1,0:T(8,128)(2,1)}, u32[]{:S(2)}, u32[]{:S(2)}) collective-permute-start(bf16[256,768]{1,0:T(8,128)(2,1)} %get-tuple-element.48), channel_id=1, source_target_pairs={{2,0},{3,1},{4,2},{5,3},{6,4},{7,5},{10,8},{11,9},{12,10},{13,11},... | collective-permute-start | bytes 1179656 | tf_op jit(solution)/shard_map/ppermute | solution.py:69
  143.4 21.2 %collective-permute-start.14 = (bf16[256,768]{1,0:T(8,128)(2,1)}, bf16[256,768]{1,0:T(8,128)(2,1)}, u32[]{:S(2)}, u32[]{:S(2)}) collective-permute-start(bf16[256,768]{1,0:T(8,128)(2,1)} %get-tuple-element.48), channel_id=1, source_target_pairs={{0,2},{1,3},{2,4},{3,5},{4,6},{5,7},{8,10},{9,11},{10,12},{11,13},... | collective-permute-start | bytes 1179656 | tf_op jit(solution)/shard_map/ppermute | solution.py:64
  152.9 14.9 %collective-permute-start.31 = (bf16[1,2,192,1024]{3,2,1,0:T(8,128)(2,1)}, bf16[1,2,192,1024]{3,2,1,0:T(8,128)(2,1)}, u32[]{:S(2)}, u32[]{:S(2)}) collective-permute-start(bf16[1,2,192,1024]{3,2,1,0:T(8,128)(2,1)} %fusion.10), channel_id=1, source_target_pairs={{0,8},{8,0},{16,24},{24,16},{1,9},{9,1},{17,25},{25,17},{2,10},{10... | collective-permute-start | bytes 2359304 | tf_op jit(solution)/shard_map/ppermute | solution.py:91
  155.0 16.1 %all-to-all-start.1 = ((bf16[2,32,4,768]{3,2,0,1:T(4,128)(2,1)}), bf16[2,32,4,768]{3,2,0,1:T(4,128)(2,1)S(1)}, u32[]{:S(2)}, u32[]{:S(2)}) async-start(bf16[2,32,4,768]{3,2,0,1:T(4,128)(2,1)} %pad_maximum_fusion.1), calls=%async_computation.1 | async-start | bytes 786432 | tf_op jit(solution)/shard_map/all_to_all | solution.py:40
  164.4 48.7 %collective-permute-start.26 = (bf16[2,2,192,1024]{3,2,1,0:T(8,128)(2,1)}, bf16[2,2,192,1024]{3,2,1,0:T(8,128)(2,1)}, u32[]{:S(2)}, u32[]{:S(2)}) collective-permute-start(bf16[2,2,192,1024]{3,2,1,0:T(8,128)(2,1)} %fusion), channel_id=1, source_target_pairs={{0,8},{8,0},{16,24},{24,16},{1,9},{9,1},{17,25},{25,17},{2,10},{10... | collective-permute-start | bytes 4718600 | tf_op jit(solution)/shard_map/ppermute | solution.py:91
  164.6 51.4 %collective-permute-start.18 = (bf16[256,768]{1,0:T(8,128)(2,1)}, bf16[256,768]{1,0:T(8,128)(2,1)}, u32[]{:S(2)}, u32[]{:S(2)}) collective-permute-start(bf16[256,768]{1,0:T(8,128)(2,1)} %collective-permute-done.14), channel_id=1, source_target_pairs={{2,3},{3,2},{4,5},{5,4},{6,7},{7,6},{10,11},{11,10},{12,13},{13,12... | collective-permute-start | bytes 1179656 | tf_op jit(solution)/shard_map/ppermute | solution.py:59
  169.3 11.5 %collective-permute-start.32 = (bf16[1,1,192,1024]{3,2,1,0:T(8,128)(2,1)S(1)}, bf16[1,1,192,1024]{3,2,1,0:T(8,128)(2,1)}, u32[]{:S(2)}, u32[]{:S(2)}) collective-permute-start(bf16[1,1,192,1024]{3,2,1,0:T(8,128)(2,1)S(1)} %dynamic-slice_convert_fusion.4), channel_id=1, source_target_pairs={{0,16},{8,24},{16,0},{24,8},{1,17},{9,25},{17,1},{25,9},{2,18},{10... | collective-permute-start | bytes 1179656 | tf_op jit(solution)/shard_map/ppermute | solution.py:91
  171.4 33.2 %collective-permute-start.20 = (bf16[256,768]{1,0:T(8,128)(2,1)}, bf16[256,768]{1,0:T(8,128)(2,1)S(1)}, u32[]{:S(2)}, u32[]{:S(2)}) collective-permute-start(bf16[256,768]{1,0:T(8,128)(2,1)} %collective-permute-done.14), channel_id=1, source_target_pairs={{2,4},{3,5},{4,6},{5,7},{10,12},{11,13},{12,14},{13,15},{18,20},{1... | collective-permute-start | bytes 1179656 | tf_op jit(solution)/shard_map/ppermute | solution.py:64
  172.1 19.6 %collective-permute-start.16 = (bf16[256,768]{1,0:T(8,128)(2,1)}, bf16[256,768]{1,0:T(8,128)(2,1)S(1)}, u32[]{:S(2)}, u32[]{:S(2)}) collective-permute-start(bf16[256,768]{1,0:T(8,128)(2,1)} %collective-permute-done.15), channel_id=1, source_target_pairs={{2,0},{3,1},{4,2},{5,3},{10,8},{11,9},{12,10},{13,11},{18,16},{19,... | collective-permute-start | bytes 1179656 | tf_op jit(solution)/shard_map/ppermute | solution.py:69
  191.7 18.5 %collective-permute-start.37 = (bf16[2,1,192,1024]{3,2,1,0:T(8,128)(2,1)S(1)}, bf16[2,1,192,1024]{3,2,1,0:T(8,128)(2,1)S(1)}, u32[]{:S(2)}, u32[]{:S(2)}) collective-permute-start(bf16[2,1,192,1024]{3,2,1,0:T(8,128)(2,1)S(1)} %dynamic-slice_convert_fusion.2), channel_id=1, source_target_pairs={{0,16},{8,24},{16,0},{24,8},{1,17},{9,25},{17,1},{25,9},{2,18},{10... | collective-permute-start | bytes 2359304 | tf_op jit(solution)/shard_map/ppermute | solution.py:91
  204.6 31.7 %collective-permute-start.25 = (bf16[256,768]{1,0:T(8,128)(2,1)}, bf16[256,768]{1,0:T(8,128)(2,1)S(1)}, u32[]{:S(2)}, u32[]{:S(2)}) collective-permute-start(bf16[256,768]{1,0:T(8,128)(2,1)} %collective-permute-done.15), channel_id=1, source_target_pairs={{0,1},{1,0},{2,3},{3,2},{4,5},{5,4},{8,9},{9,8},{10,11},{11,10},{1... | collective-permute-start | bytes 1179656 | tf_op jit(solution)/shard_map/ppermute | solution.py:59
  210.2 16.5 %collective-permute-start.19 = (bf16[256,768]{1,0:T(8,128)(2,1)S(1)}, bf16[256,768]{1,0:T(8,128)(2,1)S(1)}, u32[]{:S(2)}, u32[]{:S(2)}) collective-permute-start(bf16[256,768]{1,0:T(8,128)(2,1)S(1)} %collective-permute-done.17), channel_id=1, source_target_pairs={{0,1},{1,0},{8,9},{9,8},{16,17},{17,16},{24,25},{25,24}} | collective-permute-start | bytes 1179656 | tf_op jit(solution)/shard_map/ppermute | solution.py:59
  213.1 14.7 %collective-permute-start.21 = (bf16[256,768]{1,0:T(8,128)(2,1)S(1)}, bf16[256,768]{1,0:T(8,128)(2,1)S(1)}, u32[]{:S(2)}, u32[]{:S(2)}) collective-permute-start(bf16[256,768]{1,0:T(8,128)(2,1)S(1)} %collective-permute-done.20), channel_id=1, source_target_pairs={{4,5},{5,4},{6,7},{7,6},{12,13},{13,12},{14,15},{15,14},{20,21},{2... | collective-permute-start | bytes 1179656 | tf_op jit(solution)/shard_map/ppermute | solution.py:59
  216.0 19.1 %collective-permute-start.22 = (bf16[256,768]{1,0:T(8,128)(2,1)S(1)}, bf16[256,768]{1,0:T(8,128)(2,1)S(1)}, u32[]{:S(2)}, u32[]{:S(2)}) collective-permute-start(bf16[256,768]{1,0:T(8,128)(2,1)S(1)} %collective-permute-done.16), channel_id=1, source_target_pairs={{0,1},{1,0},{2,3},{3,2},{8,9},{9,8},{10,11},{11,10},{16,17},{17,16... | collective-permute-start | bytes 1179656 | tf_op jit(solution)/shard_map/ppermute | solution.py:59
  219.3 17.0 %collective-permute-start.24 = (bf16[256,768]{1,0:T(8,128)(2,1)S(1)}, bf16[256,768]{1,0:T(8,128)(2,1)S(1)}, u32[]{:S(2)}, u32[]{:S(2)}) collective-permute-start(bf16[256,768]{1,0:T(8,128)(2,1)S(1)} %collective-permute-done.23), channel_id=1, source_target_pairs={{6,7},{7,6},{14,15},{15,14},{22,23},{23,22},{30,31},{31,30}} | collective-permute-start | bytes 1179656 | tf_op jit(solution)/shard_map/ppermute | solution.py:59
  226.7 13.3 %collective-permute-start.38 = (bf16[384,512]{1,0:T(8,128)(2,1)S(1)}, bf16[384,512]{1,0:T(8,128)(2,1)S(1)}, u32[]{:S(2)}, u32[]{:S(2)}) collective-permute-start(bf16[384,512]{1,0:T(8,128)(2,1)S(1)} %select_convert_fusion), channel_id=1, source_target_pairs={{0,1},{1,0},{2,3},{3,2},{4,5},{5,4},{6,7},{7,6},{8,9},{9,8},{10,11... | collective-permute-start | bytes 1179656 | tf_op jit(solution)/shard_map/ppermute | solution.py:91
  227.8 12.5 %collective-permute-start.27 = (bf16[2,1,192,1024]{3,2,1,0:T(8,128)(2,1)S(1)}, bf16[2,1,192,1024]{3,2,1,0:T(8,128)(2,1)S(1)}, u32[]{:S(2)}, u32[]{:S(2)}) collective-permute-start(bf16[2,1,192,1024]{3,2,1,0:T(8,128)(2,1)S(1)} %dynamic-slice_convert_fusion.3), channel_id=1, source_target_pairs={{0,16},{8,24},{16,0},{24,8},{1,17},{9,25},{17,1},{25,9},{2,18},{10... | collective-permute-start | bytes 2359304 | tf_op jit(solution)/shard_map/ppermute | solution.py:91
  (43 other events, 491.5 us)

commit v2 on v0

--- a/solution.py
+++ b/solution.py
@@ -1,6 +1,8 @@
 import jax
 import jax.numpy as jnp
 from jax import lax
+from jax.experimental import pallas as pl
+from jax.experimental.pallas import tpu as pltpu
 from jax.sharding import PartitionSpec as P
 
 
@@ -39,6 +41,309 @@
     width = stacked.shape[-1]
     arrived = lax.all_to_all(stacked, ("row", "col"), split_axis=1, concat_axis=1, tiled=True)
     return (arrived[0].reshape(-1, width), arrived[1].reshape(-1, width))
+
+
+def flip(index, bit):
+    return index + bit - 2 * bit * ((index // bit) % 2)
+
+
+def axis_bits(axis):
+    return [(axis, 1 << b) for b in range(lax.axis_size(axis).bit_length() - 1)]
+
+
+class Line:
+    def __init__(self, block, got, up, down, cross, landed):
+        self.block, self.got, self.landed = block, got, landed
+        self.up, self.down, self.cross = up, down, cross
+        self.me = lax.axis_index("col")
+        self.depth = lax.axis_size("col") // 2
+        self.level = self.me // 2
+        self.has_up = self.level + 1 < self.depth
+        self.has_down = self.level > 0
+
+    def copy(self, source, slot, target, send):
+        return pltpu.make_async_remote_copy(
+            src_ref=source,
+            dst_ref=self.got.at[slot],
+            send_sem=send.at[slot],
+            recv_sem=self.landed.at[slot],
+            device_id={"col": target},
+            device_id_type=pl.DeviceIdType.MESH,
+        )
+
+    def go_up(self, source, slot):
+        return self.copy(source, slot, self.me + 2, self.up)
+
+    def go_down(self, source, slot):
+        return self.copy(source, slot, self.me - 2, self.down)
+
+    def go_across(self, source, slot):
+        return self.copy(source, slot, flip(self.me, 1), self.cross)
+
+    def first(self):
+        @pl.when(self.has_up)
+        def _():
+            self.go_up(self.block, self.me).start()
+
+        @pl.when(self.has_down)
+        def _():
+            self.go_down(self.block, self.me).start()
+
+        self.go_across(self.block, self.me).start()
+        self.got[self.me] = self.block[...]
+
+    def hop(self, step):
+        @pl.when(self.level >= step)
+        def _():
+            slot = self.me - 2 * step
+            held = self.got.at[slot]
+            self.go_across(held, slot).wait_recv()
+
+            @pl.when(self.has_up)
+            def _():
+                self.go_up(held, slot).start()
+
+            self.go_across(held, slot).start()
+
+        @pl.when(self.level + step < self.depth)
+        def _():
+            slot = self.me + 2 * step
+            held = self.got.at[slot]
+            self.go_across(held, slot).wait_recv()
+
+            @pl.when(self.has_down)
+            def _():
+                self.go_down(held, slot).start()
+
+            self.go_across(held, slot).start()
+
+    def finish(self):
+        for pair in range(self.depth):
+            slot = 2 * pair + 1 - self.me % 2
+            self.go_across(self.got.at[slot], slot).wait_recv()
+            mine = 2 * pair + self.me % 2
+            self.go_across(self.block, mine).wait_send()
+
+            @pl.when((pair <= self.level) & self.has_up)
+            def _():
+                self.go_up(self.block, mine).wait_send()
+
+            @pl.when((pair >= self.level) & self.has_down)
+            def _():
+                self.go_down(self.block, mine).wait_send()
+
+
+def greet(line, partners):
+    barrier = pltpu.get_barrier_semaphore()
+    for axis, bit in partners:
+        pl.semaphore_signal(
+            barrier,
+            inc=1,
+            device_id={axis: flip(lax.axis_index(axis), bit)},
+            device_id_type=pl.DeviceIdType.MESH,
+        )
+
+    @pl.when(line.has_up)
+    def _():
+        pl.semaphore_signal(
+            barrier, inc=1, device_id={"col": line.me + 2}, device_id_type=pl.DeviceIdType.MESH
+        )
+
+    @pl.when(line.has_down)
+    def _():
+        pl.semaphore_signal(
+            barrier, inc=1, device_id={"col": line.me - 2}, device_id_type=pl.DeviceIdType.MESH
+        )
+
+    ends = line.has_up.astype(jnp.int32) + line.has_down.astype(jnp.int32)
+    pl.semaphore_wait(barrier, len(partners) + ends)
+
+
+def gather_kernel(block, got, up, down, cross, landed):
+    line = Line(block, got, up, down, cross, landed)
+    greet(line, [("col", 1)])
+    line.first()
+    for step in range(1, line.depth):
+        line.hop(step)
+    line.finish()
+
+
+def line_semaphores():
+    return [pltpu.SemaphoreType.DMA((lax.axis_size("col"),)) for _ in range(4)]
+
+
+def gather_blocks(block):
+    size = lax.axis_size("col")
+    return pl.pallas_call(
+        gather_kernel,
+        out_shape=jax.ShapeDtypeStruct((size,) + block.shape, block.dtype),
+        in_specs=[pl.BlockSpec(memory_space=pltpu.VMEM)],
+        out_specs=pl.BlockSpec(memory_space=pltpu.VMEM),
+        scratch_shapes=line_semaphores(),
+        compiler_params=pltpu.CompilerParams(
+            collective_id=0, has_side_effects=True, vmem_limit_bytes=24 * 2**20
+        ),
+    )(block)
+
+
+def halving_counts(size):
+    counts, left = [], size
+    while left > 1:
+        left //= 2
+        counts.append(left)
+    return counts
+
+
+def backward_kernel(
+    block, partial, got, total, up, down, cross, landed, sent, heard, acc_rows, acc, *buffers
+):
+    line = Line(block, got, up, down, cross, landed)
+    row_stages = axis_bits("row")
+    stages = row_stages + axis_bits("col")
+    greet(line, stages)
+    line.first()
+    count = len(stages)
+    send_buf, recv_buf = buffers[:count], buffers[count:]
+    matrices, rows = partial.shape[:2]
+    columns = lax.axis_size("col")
+    width = total.shape[2]
+
+    def copy(stage, matrix):
+        axis, bit = stages[stage]
+        return pltpu.make_async_remote_copy(
+            src_ref=send_buf[stage].at[matrix],
+            dst_ref=recv_buf[stage].at[matrix],
+            send_sem=sent.at[stage, matrix],
+            recv_sem=heard.at[stage, matrix],
+            device_id={axis: flip(lax.axis_index(axis), bit)},
+            device_id_type=pl.DeviceIdType.MESH,
+        )
+
+    mine = lax.axis_index("row") % 2
+
+    @pl.loop(0, matrices)
+    def _(matrix):
+        @pl.loop(0, rows // 2)
+        def _(k):
+            send_buf[0][matrix, k] = partial[matrix, 2 * k + 1 - mine].astype(jnp.bfloat16)
+
+        copy(0, matrix).start()
+
+        @pl.loop(0, rows // 2)
+        def _(k):
+            acc_rows[matrix, k] = partial[matrix, 2 * k + mine]
+
+    def add_rows(stage, matrix, keep):
+        @pl.loop(0, send_buf[stage].shape[1])
+        def _(n):
+            at = keep(n)
+            acc_rows[matrix, at] = acc_rows[matrix, at] + recv_buf[stage][matrix, n].astype(
+                jnp.float32
+            )
+
+    def add_columns(stage, matrix, keep):
+        @pl.loop(0, send_buf[stage].shape[1])
+        def _(n):
+            at = keep(n)
+            acc[matrix, at] = acc[matrix, at] + recv_buf[stage][matrix, n].astype(jnp.float32)
+
+    def split_columns(stage, matrix, keep):
+        for c in range(columns):
+            part = pl.ds(c * width, width)
+            acc[matrix, c] = acc_rows[matrix, keep(0), :, part] + recv_buf[stage][
+                matrix, 0, :, part
+            ].astype(jnp.float32)
+
+    hops = list(range(1, line.depth))
+    if hops:
+        line.hop(hops.pop(0))
+    keep, start, step = (lambda n: n), 0, 1
+    for stage in range(1, count):
+        axis, bit = stages[stage]
+        mine = (lax.axis_index(axis) // bit) % 2
+        if stage < len(row_stages):
+            add, values = add_rows, acc_rows
+        elif stage == len(row_stages):
+            add, values = split_columns, acc
+            start, step = 0, 1
+        else:
+            add, values = add_columns, acc
+
+        def place(n, side, start=start, step=step):
+            return start + side * step + n * 2 * step
+
+        @pl.loop(0, matrices)
+        def _(matrix):
+            copy(stage - 1, matrix).wait_recv()
+            add(stage - 1, matrix, keep)
+
+            @pl.loop(0, send_buf[stage].shape[1])
+            def _(n):
+                send_buf[stage][matrix, n] = values[matrix, place(n, 1 - mine)].astype(
+                    jnp.bfloat16
+                )
+
+            copy(stage, matrix).start()
+
+        keep = lambda n, place=place, mine=mine: place(n, mine)
+        start, step = start + mine * step, 2 * step
+        if stage == 1:
+            while hops:
+                line.hop(hops.pop(0))
+
+    @pl.loop(0, matrices)
+    def _(matrix):
+        copy(count - 1, matrix).wait_recv()
+        total[matrix] = acc[matrix, keep(0)] + recv_buf[count - 1][matrix, 0].astype(jnp.float32)
+        for stage in range(count):
+            copy(stage, matrix).wait_send()
+
+    line.finish()
+
+
+def gather_and_scatter(block, partial):
+    rows, size = lax.axis_size("row"), lax.axis_size("col")
+    matrices, depth, wide = partial.shape
+    high, width = depth // rows, wide // size
+    buffers = [
+        pltpu.VMEM((matrices, n, high, wide), jnp.bfloat16) for n in halving_counts(rows)
+    ] + [pltpu.VMEM((matrices, n, high, width), jnp.bfloat16) for n in halving_counts(size)]
+    vmem = pl.BlockSpec(memory_space=pltpu.VMEM)
+    return pl.pallas_call(
+        backward_kernel,
+        out_shape=(
+            jax.ShapeDtypeStruct((size,) + block.shape, block.dtype),
+            jax.ShapeDtypeStruct((matrices, high, width), jnp.float32),
+        ),
+        in_specs=[vmem, vmem],
+        out_specs=(vmem, vmem),
+        scratch_shapes=line_semaphores()
+        + [pltpu.SemaphoreType.DMA((len(buffers), matrices)) for _ in range(2)]
+        + [
+            pltpu.VMEM((matrices, rows // 2, high, wide), jnp.float32),
+            pltpu.VMEM((matrices, size, high, width), jnp.float32),
+        ]
+        + buffers
+        + buffers,
+        compiler_params=pltpu.CompilerParams(
+            collective_id=1, has_side_effects=True, vmem_limit_bytes=56 * 2**20
+        ),
+    )(block, partial.reshape(matrices, rows, high, wide))
+
+
+def listed_rows(entries, width):
+    turned = entries.T
+    high = jnp.floor_divide(turned, 256)
+    low = turned - 256 * high
+    both = jnp.concatenate([high, low], axis=1).astype(jnp.bfloat16)
+    return jnp.pad(both, ((0, 0), (0, width - both.shape[1])))
+
+
+def match_listed(entries, wanted):
+    accum = jnp.zeros((wanted.shape[0], entries.shape[1]), jnp.float32)
+    for slot in range(entries.shape[0]):
+        accum = accum + (entries[slot][None, :] == wanted[:, None]).astype(jnp.float32)
+    return accum.astype(jnp.bfloat16)
 
 
 def per_device(
@@ -58,11 +363,19 @@
     papers = x_paper.shape[0]
     authors = x_author.shape[0]
     cnt_cite = jnp.maximum(jnp.sum((cite_nbr >= 0).astype(jnp.float32), axis=1, keepdims=True), 1.0)
-    rows_in = lax.all_gather(x_paper, "col", axis=0, tiled=True)
+    width = x_paper.shape[1]
+    gathered = gather_blocks(
+        jnp.concatenate([x_paper, listed_rows(cite_nbr, width)], axis=0)
+    )
+    rows_in = gathered[:, :papers].reshape(-1, width)
+    lists = gathered[:, papers:].astype(jnp.int32)
+    entries = 256 * lists[:, :, :papers] + lists[:, :, papers : 2 * papers]
+    entries = jnp.transpose(entries, (1, 0, 2)).reshape(entries.shape[1], -1)
+    positions = lax.iota(jnp.int32, papers)
     columns = lax.iota(jnp.int32, rows_in.shape[0])
-    cite_total = jnp.dot(
-        match_table(cite_nbr, columns), rows_in, preferred_element_type=jnp.float32
-    )
+    table_cite = match_table(cite_nbr, columns)
+    table_cited = match_listed(entries, lax.axis_index("col") * papers + positions)
+    cite_total = jnp.dot(table_cite, rows_in, preferred_element_type=jnp.float32)
     cited = (cite_total / cnt_cite).astype(jnp.bfloat16)
     send_list = write_src[0]
     take_list = write_dst[0]
@@ -98,12 +411,18 @@
     dz_cite = (project_back(dpre_paper, w_cite) / cnt_cite).astype(jnp.bfloat16)
     dz_write = (project_back(dpre_paper, w_write) / cnt_write).astype(jnp.bfloat16)
     dz_written = (project_back(dpre_author, w_written) / cnt_written).astype(jnp.bfloat16)
-    columns = lax.iota(jnp.int32, lax.axis_size("col") * papers)
-    cite_grad = lax.psum_scatter(
-        contract_rows(match_table(cite_nbr, columns), dz_cite),
-        "col",
-        scatter_dimension=0,
-        tiled=True,
+    local_grads = jnp.stack(
+        [
+            contract_rows(x_paper, dpre_paper),
+            contract_rows(cited, dpre_paper),
+            contract_rows(written, dpre_paper),
+            contract_rows(x_author, dpre_author),
+            contract_rows(authored, dpre_author),
+        ]
+    )
+    dz_rows, summed = gather_and_scatter(dz_cite, local_grads)
+    cite_grad = jnp.dot(
+        table_cited, dz_rows.reshape(-1, width), preferred_element_type=jnp.float32
     )
     back_papers, back_authors = edge_rows(
         select_rows(dz_written, send_list), select_rows(dz_write, take_list)
@@ -117,17 +436,6 @@
         project_back(dpre_author, w_self_author)
         + jnp.dot(table_author, back_authors, preferred_element_type=jnp.float32)
     ).astype(jnp.bfloat16)
-    local_grads = jnp.stack(
-        [
-            contract_rows(x_paper, dpre_paper),
-            contract_rows(cited, dpre_paper),
-            contract_rows(written, dpre_paper),
-            contract_rows(x_author, dpre_author),
-            contract_rows(authored, dpre_author),
-        ]
-    )
-    halfway = lax.psum_scatter(local_grads, "row", scatter_dimension=1, tiled=True)
-    summed = lax.psum_scatter(halfway, "col", scatter_dimension=2, tiled=True)
     devices_all = lax.axis_size("row") * lax.axis_size("col")
     paper_scale = float(papers * devices_all) ** (-0.5)
     author_scale = float(authors * devices_all) ** (-0.5)

time: 511 us -> 230 us (0.45)
  waiting for transfers between devices: 362 us -> 0.01 us
  Pallas kernels: 0 us -> 134 us
  local copies, waits for them, and re-layouts: 66.5 us -> 29.7 us
  between operations: 14.1 us -> 1.08 us
    reduce_scatter x2 -> x0, waiting for transfers between devices: 179 us -> none  [the longest x1 102 us: per_device(): summed = lax.psum_scatter(halfway, 'col', scatter_dimension=2, tiled=True)]
    pallas_call x0 -> x2, Pallas kernels: none -> 134 us  [the longest x1 83 us: gather_and_scatter(): pl.pallas_call(backward_kernel, out_shape=(jax.ShapeDtypeStruct((size,) +...]
    unnamed x5 -> x0, waiting for transfers between devices: 111 us -> none
    unnamed x39 -> x76, local copies, waits for them, and re-layouts: 59.4 us -> 15.6 us
    all_to_all x2, waiting for transfers between devices: 40.8 us -> 0.01 us  [edge_rows(): lax.all_to_all(stacked, ('row', 'col'), split_axis=1, concat_axis=1, tile...]
    all_gather x1 -> x0, waiting for transfers between devices: 30.5 us -> none  [per_device(): rows_in = lax.all_gather(x_paper, 'col', axis=0, tiled=True)]
    dot_general x6 -> x5, matrix products: 20 us -> 11.4 us  [contract_rows(): lax.dot_general(left_side, right_side, (((0,), (0,)), ((), ())), preferre...]
    dot_general x1 -> x2, matrix products: 6.87 us -> 13.6 us  [the longest x1 7.63 us: per_device(): jnp.dot(table_cite, rows_in, preferred_element_type=jnp.float32)]
  transfers between devices with their start and end apart: 6 -> 2, of which waited for: 6 -> 0; matrix products, arithmetic and copies ran while one was open for 11% -> 17% of each run, Pallas kernels for 0% -> 58%
where the time goes in v2:
time: 230 us; the launch traced here: 229 us
  Pallas kernels  134 us (58%)
  matrix products  44 us (19%)
  local copies, waits for them, and re-layouts  29.7 us (13%)
  other arithmetic  10.7 us (5%)
  starting transfers between devices  10 us (4%)
    pallas_call x1, Pallas kernels, gather_and_scatter(): pl.pallas_call(backward_kernel, out_shape=(jax.ShapeDtypeStruct((size,) +...  83 us
    pallas_call x1, Pallas kernels, gather_blocks(): pl.pallas_call(gather_kernel, out_shape=jax.ShapeDtypeStruct((size,) + bl...  50.8 us
    unnamed x76, local copies, waits for them, and re-layouts  15.6 us
    dot_general x5, matrix products, contract_rows(): lax.dot_general(left_side, right_side, (((0,), (0,)), ((), ())), preferre...  11.4 us
    all_to_all x2, starting transfers between devices, edge_rows(): lax.all_to_all(stacked, ('row', 'col'), split_axis=1, concat_axis=1, tile...  10 us
    dot_general x1, matrix products, per_device(): jnp.dot(table_cite, rows_in, preferred_element_type=jnp.float32)  7.63 us
    dot_general x1, matrix products, per_device(): jnp.dot(table_cited, dz_rows.reshape(-1, width), preferred_element_type=j...  5.99 us
    dot_general x5, matrix products, project_back(): lax.dot_general(delta, weight, (((1,), (1,)), ((), ())), preferred_elemen...  5.89 us
  transfers between devices with their start and end apart: 2, of which 0 were waited for; matrix products, arithmetic and copies ran while one was open for 17% of the time, Pallas kernels for 58%

profile of v2, /device:TPU:0, one launch (start us, length us, event | category | flops | bytes accessed | tf_op | source)
XLA Modules:
  0.0 229.4 jit_solution(13479763707107807668)
XLA Ops:
  3.9 2.0 gather_fusion.1
  7.5 1.0 pad_maximum_fusion.1
  8.5 7.4 %all-to-all-start = ((bf16[2,32,4,768]{3,2,0,1:T(4,128)(2,1)}), bf16[2,32,4,768]{3,2,0,1:T(4,128)(2,1)}, u32[]{:S(2)}, u32[]{:S(2)}) async-start(bf16[2,32,4,768]{3,2,0,1:T(4,128)(2,1)} %pad_maximum_fusion.1), calls=%async_computation | async-start | bytes 786432 | tf_op jit(solution)/shard_map/all_to_all | solution.py:42
  16.9 50.8 %shard_map.164 = bf16[8,272,768]{2,1,0:T(8,128)(2,1)S(1)} custom-call(bf16[272,768]{1,0:T(8,128)(2,1)S(1)} %pad_maximum_fusion.block), custom_call_target="tpu_custom_call" | custom-call | tf_op jit(solution)/shard_map/pallas_call | solution.py:177
  67.7 1.8 slice.152
  74.1 7.6 %fusion.7 = bf16[256,768]{1,0:T(8,128)(2,1)} fusion(bf16[2048,768]{1,0:T(8,128)(2,1)} %bitcast.129, s32[256]{0:T(256)} %bitcast.147, s32[256]{0:T(256)} %bitcast.148, s32[256]{0:T(256)} %bitcast.149, s32[256]{0:T(256)} %bitcast.150, s32[256]{0:T(256)} %bitcast.151, s32[256]{0:T(256)} %bitcast.152, s32[256]{0:T(256)} %bitcast.153, s32[256]{0:T(256)} %bitcast.154, ...), kind=kOutput, calls=%fused_computation.41 | convolution fusion | flops 830865408 | bytes 3556352 | tf_op jit(solution)/shard_map/dot_general | solution.py:378
  82.8 3.0 %fusion.62 = f32[256,1024]{1,0:T(8,128)} fusion(bf16[256,768]{1,0:T(8,128)(2,1)S(1)} %copy-done.3, bf16[768,1024]{1,0:T(8,128)(2,1)} %param.21), kind=kOutput, calls=%fused_computation.141 | convolution fusion | flops 402653184 | bytes 3014656 | tf_op jit(solution)/shard_map/dot_general | solution.py:404
  85.8 1.6 convolution_add_fusion.2
  87.4 1.2 fusion.58
  88.6 1.1 fusion
  90.0 1.7 multiply_convert_fusion.1
  91.7 2.2 fusion.63
  94.0 2.2 fusion.64
  96.2 2.3 %fusion.65 = f32[768,1024]{1,0:T(8,128)} fusion(bf16[256,768]{1,0:T(8,128)(2,1)S(1)} %fusion, bf16[256,1024]{1,0:T(8,128)(2,1)S(1)} %get-tuple-element.11), kind=kOutput, calls=%fused_computation.144 | convolution fusion | flops 402653184 | bytes 4063232 | tf_op jit(solution)/shard_map/dot_general | solution.py:29
  98.9 1.1 copy-done.31
  100.1 2.9 %multiply_convert_fusion = (bf16[256,1024]{1,0:T(8,128)(2,1)S(1)}, bf16[256,1024]{1,0:T(8,128)(2,1)}) fusion(bf16[256,1024]{1,0:T(8,128)(2,1)S(1)} %copy-done.33, f32[256,1024]{1,0:T(8,128)} %fusion.62, bf16[256,768]{1,0:T(8,128)(2,1)S(1)} %fusion.1, bf16[768,1024]{1,0:T(8,128)(2,1)S(1)} %copy-done.31), kind=kOutput, calls=%fused_computation.43 | convolution fusion | flops 406061056 | bytes 4587520 | tf_op jit(solution)/shard_map/dot_general | solution.py:404
  103.0 2.3 %fusion.66 = f32[1024,768]{0,1:T(8,128)} fusion(bf16[256,1024]{1,0:T(8,128)(2,1)S(1)} %get-tuple-element.9, bf16[256,768]{1,0:T(8,128)(2,1)S(1)} %copy-done.3), kind=kOutput, calls=%fused_computation.145 | convolution fusion | flops 402653184 | bytes 4063232 | tf_op jit(solution)/shard_map/dot_general | solution.py:29
  105.4 2.3 fusion.67
  107.6 1.6 fusion.2.block
  110.5 1.3 copy-done.7
  111.8 1.8 constant_dynamic-update-slice_fusion.4
  116.9 2.6 %all-to-all-start.1 = ((bf16[2,32,4,768]{3,2,0,1:T(4,128)(2,1)}), bf16[2,32,4,768]{3,2,0,1:T(4,128)(2,1)S(1)}, u32[]{:S(2)}, u32[]{:S(2)}) async-start(bf16[2,32,4,768]{3,2,0,1:T(4,128)(2,1)} %pad_maximum_fusion.2), calls=%async_computation.1 | async-start | bytes 786432 | tf_op jit(solution)/shard_map/all_to_all | solution.py:42
  119.5 4.2 %constant_dynamic-update-slice_fusion.3 = f32[5,4,192,1024]{3,2,1,0:T(8,128)} fusion(f32[5,4,192,1024]{3,2,1,0:T(8,128)} %constant_dynamic-update-slice_fusion.4, f32[1,4,192,1024]{3,2,1,0:T(8,128)} %bitcast.125), kind=kLoop, calls=%fused_computation.123 | loop fusion | bytes 6291456
  123.6 1.9 constant_dynamic-update-slice_fusion.2
  125.6 1.1 copy-done.6
  126.7 1.9 constant_dynamic-update-slice_fusion.1
  128.6 1.1 copy-done.5
  129.7 1.8 constant_dynamic-update-slice_fusion.partial
  131.5 83.0 %shard_map.165 = (bf16[8,256,768]{2,1,0:T(8,128)(2,1)}, f32[5,192,128]{2,1,0:T(8,128)}) custom-call(bf16[256,768]{1,0:T(8,128)(2,1)} %fusion.2.block, f32[5,4,192,1024]{3,2,1,0:T(8,128)} %constant_dynamic-update-slice_fusion.partial), custom_call_target="tpu_custom_call" | custom-call | tf_op jit(solution)/shard_map/pallas_call | solution.py:312
  214.6 6.0 %fusion.8 = f32[256,768]{1,0:T(8,128)S(1)} fusion(bf16[2048,768]{1,0:T(8,128)(2,1)} %bitcast.162, s32[2048]{0:T(1024)S(1)} %bitcast.131, s32[2048]{0:T(1024)S(1)} %bitcast.132, s32[2048]{0:T(1024)S(1)} %bitcast.133, s32[2048]{0:T(1024)S(1)} %bitcast.134, s32[2048]{0:T(1024)S(1)} %bitcast.135, s32[2048]{0:T(1024)S(1)} %bitcast.136, s32[2048]{0:T(1024)S(1)} %bitcast.137, ...), kind=kOutput, calls=%fused_computation.42 | convolution fusion | flops 830472192 | bytes 4064256 | tf_op jit(solution)/shard_map/dot_general | solution.py:424
  221.5 1.5 fusion.68
  223.0 1.6 convolution_add_fusion.5
  (121 shorter events, 22.2 us)
Async XLA Ops:
  0.6 89.1 %copy-start = (bf16[768,1024]{1,0:T(8,128)(2,1)S(1)}, bf16[768,1024]{1,0:T(8,128)(2,1)}, u32[]{:S(2)}) copy-start(bf16[768,1024]{1,0:T(8,128)(2,1)} %param.20) | copy-start | bytes 4718596
  0.6 5.5 %copy-start.3 = (bf16[256,768]{1,0:T(8,128)(2,1)S(1)}, bf16[256,768]{1,0:T(8,128)(2,1)}, u32[]{:S(2)}) copy-start(bf16[256,768]{1,0:T(8,128)(2,1)} %param.14) | copy-start | bytes 1179652
  6.1 9.8 %copy-start.19 = (s32[256,16]{0,1:T(8,128)S(1)}, s32[256,16]{0,1:T(8,128)}, u32[]{:S(2)}) copy-start(s32[256,16]{0,1:T(8,128)} %param.15) | copy-start | bytes 49156
  6.1 10.5 %copy-start.20 = (s32[1,32,4]{1,2,0:T(4,128)S(1)}, s32[1,32,4]{1,2,0:T(4,128)}, u32[]{:S(2)}) copy-start(s32[1,32,4]{1,2,0:T(4,128)} %param.17) | copy-start | bytes 1540
  6.1 10.6 %copy-start.21 = (s32[1,32,4]{1,2,0:T(4,128)S(1)}, s32[1,32,4]{1,2,0:T(4,128)}, u32[]{:S(2)}) copy-start(s32[1,32,4]{1,2,0:T(4,128)} %param.16) | copy-start | bytes 1540
  6.2 10.7 %copy-start.2 = (bf16[256,768]{1,0:T(8,128)(2,1)S(1)}, bf16[256,768]{1,0:T(8,128)(2,1)}, u32[]{:S(2)}) copy-start(bf16[256,768]{1,0:T(8,128)(2,1)} %param.13) | copy-start | bytes 1179652
  8.5 78.8 %all-to-all-start = ((bf16[2,32,4,768]{3,2,0,1:T(4,128)(2,1)}), bf16[2,32,4,768]{3,2,0,1:T(4,128)(2,1)}, u32[]{:S(2)}, u32[]{:S(2)}) async-start(bf16[2,32,4,768]{3,2,0,1:T(4,128)(2,1)} %pad_maximum_fusion.1), calls=%async_computation | async-start | bytes 786432 | tf_op jit(solution)/shard_map/all_to_all | solution.py:42
  67.7 3.2 %copy-start.8 = (bf16[768,1024]{1,0:T(8,128)(2,1)S(1)}, bf16[768,1024]{1,0:T(8,128)(2,1)}, u32[]{:S(2)}) copy-start(bf16[768,1024]{1,0:T(8,128)(2,1)} %param.18) | copy-start | bytes 4718596
  82.3 3.6 %copy-start.13 = (bf16[768,1024]{1,0:T(8,128)(2,1)S(1)}, bf16[768,1024]{1,0:T(8,128)(2,1)}, u32[]{:S(2)}) copy-start(bf16[768,1024]{1,0:T(8,128)(2,1)} %param.19) | copy-start | bytes 4718596
  82.3 3.6 %copy-start.15 = (bf16[256,768]{1,0:T(8,128)(2,1)S(1)}, bf16[256,768]{1,0:T(8,128)(2,1)}, u32[]{:S(2)}) copy-start(bf16[256,768]{1,0:T(8,128)(2,1)} %fusion.7) | copy-start | bytes 1179652
  91.7 2.3 copy-start.16
  96.2 2.4 %copy-start.25 = (s32[128]{0:T(128)S(1)}, s32[128]{0:T(128)}, u32[]{:S(2)}) copy-start(s32[128]{0:T(128)} %copy-done.24) | copy-start | bytes 1540
  96.2 2.4 %copy-start.29 = (f32[256]{0:T(256)S(1)}, f32[256]{0:T(256)}, u32[]{:S(2)}) copy-start(f32[256]{0:T(256)} %broadcast_maximum_fusion.2) | copy-start | bytes 3076
  98.6 1.4 copy-start.31
  98.6 1.5 copy-start.33
  105.4 2.3 copy-start.14
  105.4 2.3 copy-start.27
  107.6 1.6 copy-start.28
  109.9 1.9 copy-start.7
  116.9 107.7 %all-to-all-start.1 = ((bf16[2,32,4,768]{3,2,0,1:T(4,128)(2,1)}), bf16[2,32,4,768]{3,2,0,1:T(4,128)(2,1)S(1)}, u32[]{:S(2)}, u32[]{:S(2)}) async-start(bf16[2,32,4,768]{3,2,0,1:T(4,128)(2,1)} %pad_maximum_fusion.2), calls=%async_computation.1 | async-start | bytes 786432 | tf_op jit(solution)/shard_map/all_to_all | solution.py:42
  119.5 4.2 %copy-start.4 = (f32[768,1024]{1,0:T(8,128)S(1)}, f32[768,1024]{1,0:T(8,128)}, u32[]{:S(2)}) copy-start(f32[768,1024]{1,0:T(8,128)} %fusion.65) | copy-start | bytes 9437188
  123.6 3.0 %copy-start.6 = (f32[1024,768]{0,1:T(8,128)S(1)}, f32[1024,768]{0,1:T(8,128)}, u32[]{:S(2)}) copy-start(f32[1024,768]{0,1:T(8,128)} %fusion.66) | copy-start | bytes 9437188
  126.7 3.0 %copy-start.5 = (f32[768,1024]{1,0:T(8,128)S(1)}, f32[768,1024]{1,0:T(8,128)}, u32[]{:S(2)}) copy-start(f32[768,1024]{1,0:T(8,128)} %fusion.67) | copy-start | bytes 9437188
  131.5 83.1 %copy-start.34 = (s32[256]{0:T(256)S(1)}, s32[256]{0:T(256)}, u32[]{:S(2)}) copy-start(s32[256]{0:T(256)} %iota_add_fusion) | copy-start | bytes 3076
  214.6 6.0 %copy-start.18 = (f32[5,192,128]{2,1,0:T(8,128)S(1)}, f32[5,192,128]{2,1,0:T(8,128)}, u32[]{:S(2)}) copy-start(f32[5,192,128]{2,1,0:T(8,128)} %get-tuple-element.8) | copy-start | bytes 1474564
  214.6 6.9 %copy-start.10 = (bf16[768,1024]{1,0:T(8,128)(2,1)S(1)}, bf16[768,1024]{1,0:T(8,128)(2,1)}, u32[]{:S(2)}) copy-start(bf16[768,1024]{1,0:T(8,128)(2,1)} %param.21) | copy-start | bytes 4718596
  220.6 2.3 %copy-start.9 = (bf16[768,1024]{1,0:T(8,128)(2,1)S(1)}, bf16[768,1024]{1,0:T(8,128)(2,1)}, u32[]{:S(2)}) copy-start(bf16[768,1024]{1,0:T(8,128)(2,1)} %param.18) | copy-start | bytes 4718596
  223.0 4.4 %copy-start.23 = (s32[128]{0:T(128)S(1)}, s32[128]{0:T(128)}, u32[]{:S(2)}) copy-start(s32[128]{0:T(128)} %copy-done.22) | copy-start | bytes 1540
  223.0 6.4 %copy-start.1 = (bf16[768,1024]{1,0:T(8,128)(2,1)S(1)}, bf16[768,1024]{1,0:T(8,128)(2,1)}, u32[]{:S(2)}) copy-start(bf16[768,1024]{1,0:T(8,128)(2,1)} %param.20) | copy-start | bytes 4718596
  224.5 2.9 %copy-start.11 = (f32[256,768]{1,0:T(8,128)S(1)}, f32[256,768]{1,0:T(8,128)}, u32[]{:S(2)}) copy-start(f32[256,768]{1,0:T(8,128)} %convolution_add_fusion.5) | copy-start | bytes 2359300
  224.5 3.9 %copy-start.12 = (f32[256,768]{1,0:T(8,128)S(1)}, f32[256,768]{1,0:T(8,128)}, u32[]{:S(2)}) copy-start(f32[256,768]{1,0:T(8,128)} %fusion.68) | copy-start | bytes 2359300
  224.5 3.9 %copy-start.26 = (s32[128]{0:T(128)S(1)}, s32[128]{0:T(128)}, u32[]{:S(2)}) copy-start(s32[128]{0:T(128)} %copy-done.24) | copy-start | bytes 1540
  (5 other events, 4.7 us)

commit v3 on v2

--- a/solution.py
+++ b/solution.py
@@ -4,13 +4,6 @@
 from jax.experimental import pallas as pl
 from jax.experimental.pallas import tpu as pltpu
 from jax.sharding import PartitionSpec as P
-
-
-def match_table(entries, columns):
-    accum = jnp.zeros((entries.shape[0], columns.shape[0]), jnp.float32)
-    for slot in range(entries.shape[1]):
-        accum = accum + (entries[:, slot : slot + 1] == columns[None, :]).astype(jnp.float32)
-    return accum.astype(jnp.bfloat16)
 
 
 def select_rows(values, positions):
@@ -159,12 +152,20 @@
     pl.semaphore_wait(barrier, len(partners) + ends)
 
 
-def gather_kernel(block, got, up, down, cross, landed):
+def gather_kernel(block, entries, got, table, up, down, cross, landed):
     line = Line(block, got, up, down, cross, landed)
     greet(line, [("col", 1)])
     line.first()
-    for step in range(1, line.depth):
-        line.hop(step)
+    each = entries.shape[0]
+    for source in range(got.shape[0]):
+        wanted = source * each + lax.broadcasted_iota(jnp.int32, (each, each), 1)
+        matches = jnp.zeros((each, each), jnp.float32)
+        for slot in range(entries.shape[1]):
+            matches += (entries[:, slot : slot + 1] == wanted).astype(jnp.float32)
+        table[:, pl.ds(source * each, each)] = matches.astype(jnp.bfloat16)
+        step = source + 1
+        if step < line.depth:
+            line.hop(step)
     line.finish()
 
 
@@ -172,18 +173,22 @@
     return [pltpu.SemaphoreType.DMA((lax.axis_size("col"),)) for _ in range(4)]
 
 
-def gather_blocks(block):
+def gather_blocks(block, entries):
     size = lax.axis_size("col")
+    vmem = pl.BlockSpec(memory_space=pltpu.VMEM)
     return pl.pallas_call(
         gather_kernel,
-        out_shape=jax.ShapeDtypeStruct((size,) + block.shape, block.dtype),
-        in_specs=[pl.BlockSpec(memory_space=pltpu.VMEM)],
-        out_specs=pl.BlockSpec(memory_space=pltpu.VMEM),
+        out_shape=(
+            jax.ShapeDtypeStruct((size,) + block.shape, block.dtype),
+            jax.ShapeDtypeStruct((entries.shape[0], size * entries.shape[0]), jnp.bfloat16),
+        ),
+        in_specs=[vmem, vmem],
+        out_specs=(vmem, vmem),
         scratch_shapes=line_semaphores(),
         compiler_params=pltpu.CompilerParams(
             collective_id=0, has_side_effects=True, vmem_limit_bytes=24 * 2**20
         ),
-    )(block)
+    )(block, entries)
 
 
 def halving_counts(size):
@@ -195,7 +200,7 @@
 
 
 def backward_kernel(
-    block, partial, got, total, up, down, cross, landed, sent, heard, acc_rows, acc, *buffers
+    block, left, right, entries, got, total, table, up, down, cross, landed, sent, heard, acc_rows, acc, *buffers
 ):
     line = Line(block, got, up, down, cross, landed)
     row_stages = axis_bits("row")
@@ -204,7 +209,14 @@
     line.first()
     count = len(stages)
     send_buf, recv_buf = buffers[:count], buffers[count:]
-    matrices, rows = partial.shape[:2]
+    matrices, rows = left.shape[:2]
+    each = block.shape[0]
+
+    def product(matrix, at):
+        return jnp.dot(
+            left[matrix, at], right[matrix // 3], preferred_element_type=jnp.float32
+        )
+
     columns = lax.axis_size("col")
     width = total.shape[2]
 
@@ -225,13 +237,13 @@
     def _(matrix):
         @pl.loop(0, rows // 2)
         def _(k):
-            send_buf[0][matrix, k] = partial[matrix, 2 * k + 1 - mine].astype(jnp.bfloat16)
+            send_buf[0][matrix, k] = product(matrix, 2 * k + 1 - mine).astype(jnp.bfloat16)
 
         copy(0, matrix).start()
 
         @pl.loop(0, rows // 2)
         def _(k):
-            acc_rows[matrix, k] = partial[matrix, 2 * k + mine]
+            acc_rows[matrix, k] = product(matrix, 2 * k + mine)
 
     def add_rows(stage, matrix, keep):
         @pl.loop(0, send_buf[stage].shape[1])
@@ -288,6 +300,13 @@
         keep = lambda n, place=place, mine=mine: place(n, mine)
         start, step = start + mine * step, 2 * step
         if stage == 1:
+            wanted = line.me * each + lax.broadcasted_iota(jnp.int32, (each, each), 0)
+            for source in range(columns):
+                part = pl.ds(source * each, each)
+                matches = jnp.zeros((each, each), jnp.float32)
+                for slot in range(entries.shape[0]):
+                    matches += (entries[slot : slot + 1, part] == wanted).astype(jnp.float32)
+                table[:, part] = matches.astype(jnp.bfloat16)
             while hops:
                 line.hop(hops.pop(0))
 
@@ -301,9 +320,10 @@
     line.finish()
 
 
-def gather_and_scatter(block, partial):
+def gather_and_scatter(block, left, right, entries):
     rows, size = lax.axis_size("row"), lax.axis_size("col")
-    matrices, depth, wide = partial.shape
+    matrices, depth, each = left.shape
+    wide = right.shape[2]
     high, width = depth // rows, wide // size
     buffers = [
         pltpu.VMEM((matrices, n, high, wide), jnp.bfloat16) for n in halving_counts(rows)
@@ -314,9 +334,10 @@
         out_shape=(
             jax.ShapeDtypeStruct((size,) + block.shape, block.dtype),
             jax.ShapeDtypeStruct((matrices, high, width), jnp.float32),
+            jax.ShapeDtypeStruct((block.shape[0], entries.shape[1]), jnp.bfloat16),
         ),
-        in_specs=[vmem, vmem],
-        out_specs=(vmem, vmem),
+        in_specs=[vmem] * 4,
+        out_specs=(vmem,) * 3,
         scratch_shapes=line_semaphores()
         + [pltpu.SemaphoreType.DMA((len(buffers), matrices)) for _ in range(2)]
         + [
@@ -328,7 +349,7 @@
         compiler_params=pltpu.CompilerParams(
             collective_id=1, has_side_effects=True, vmem_limit_bytes=56 * 2**20
         ),
-    )(block, partial.reshape(matrices, rows, high, wide))
+    )(block, left.reshape(matrices, rows, high, each), right, entries)
 
 
 def listed_rows(entries, width):
@@ -337,13 +358,6 @@
     low = turned - 256 * high
     both = jnp.concatenate([high, low], axis=1).astype(jnp.bfloat16)
     return jnp.pad(both, ((0, 0), (0, width - both.shape[1])))
-
-
-def match_listed(entries, wanted):
-    accum = jnp.zeros((wanted.shape[0], entries.shape[1]), jnp.float32)
-    for slot in range(entries.shape[0]):
-        accum = accum + (entries[slot][None, :] == wanted[:, None]).astype(jnp.float32)
-    return accum.astype(jnp.bfloat16)
 
 
 def per_device(
@@ -364,17 +378,13 @@
     authors = x_author.shape[0]
     cnt_cite = jnp.maximum(jnp.sum((cite_nbr >= 0).astype(jnp.float32), axis=1, keepdims=True), 1.0)
     width = x_paper.shape[1]
-    gathered = gather_blocks(
-        jnp.concatenate([x_paper, listed_rows(cite_nbr, width)], axis=0)
+    gathered, table_cite = gather_blocks(
+        jnp.concatenate([x_paper, listed_rows(cite_nbr, width)], axis=0), cite_nbr
     )
     rows_in = gathered[:, :papers].reshape(-1, width)
     lists = gathered[:, papers:].astype(jnp.int32)
     entries = 256 * lists[:, :, :papers] + lists[:, :, papers : 2 * papers]
     entries = jnp.transpose(entries, (1, 0, 2)).reshape(entries.shape[1], -1)
-    positions = lax.iota(jnp.int32, papers)
-    columns = lax.iota(jnp.int32, rows_in.shape[0])
-    table_cite = match_table(cite_nbr, columns)
-    table_cited = match_listed(entries, lax.axis_index("col") * papers + positions)
     cite_total = jnp.dot(table_cite, rows_in, preferred_element_type=jnp.float32)
     cited = (cite_total / cnt_cite).astype(jnp.bfloat16)
     send_list = write_src[0]
@@ -411,16 +421,10 @@
     dz_cite = (project_back(dpre_paper, w_cite) / cnt_cite).astype(jnp.bfloat16)
     dz_write = (project_back(dpre_paper, w_write) / cnt_write).astype(jnp.bfloat16)
     dz_written = (project_back(dpre_author, w_written) / cnt_written).astype(jnp.bfloat16)
-    local_grads = jnp.stack(
-        [
-            contract_rows(x_paper, dpre_paper),
-            contract_rows(cited, dpre_paper),
-            contract_rows(written, dpre_paper),
-            contract_rows(x_author, dpre_author),
-            contract_rows(authored, dpre_author),
-        ]
-    )
-    dz_rows, summed = gather_and_scatter(dz_cite, local_grads)
+    left_sides = jnp.stack([x_paper.T, cited.T, written.T, x_author.T, authored.T])
+    dz_rows, summed, table_cited = gather_and_scatter(
+        dz_cite, left_sides, jnp.stack([dpre_paper, dpre_author]), entries
+    )
     cite_grad = jnp.dot(
         table_cited, dz_rows.reshape(-1, width), preferred_element_type=jnp.float32
     )

time: 230 us -> 209 us (0.909)
  matrix products: 44 us -> 21.7 us
  Pallas kernels: 134 us -> 129 us
  local copies, waits for them, and re-layouts: 29.7 us -> 32 us
    dot_general x5 -> x0, matrix products: 11.4 us -> none  [contract_rows(): lax.dot_general(left_side, right_side, (((0,), (0,)), ((), ())), preferre...]
    unnamed x76 -> x87, local copies, waits for them, and re-layouts: 15.6 us -> 10.7 us
    convert_element_type x0 -> x3, local copies, waits for them, and re-layouts: none -> 4.74 us  [the longest x1 1.91 us: per_device(): cited = (cite_total / cnt_cite).astype(jnp.bfloat16)]
    dot_general x1, matrix products: 7.63 us -> 3.66 us  [per_device(): jnp.dot(table_cite, rows_in, preferred_element_type=jnp.float32)]
    pallas_call x1, Pallas kernels: 83 us -> 79.6 us  [gather_and_scatter(): pl.pallas_call(backward_kernel, out_shape=(jax.ShapeDtypeStruct((size,) +...]
    dot_general x1, matrix products: 5.99 us -> 3.32 us  [per_device(): jnp.dot(table_cited, dz_rows.reshape(-1, width), preferred_element_type=j...]
  transfers between devices with their start and end apart: 2 -> 2, of which waited for: 0 -> 0; matrix products, arithmetic and copies ran while one was open for 17% -> 17% of each run, Pallas kernels for 58% -> 62%
where the time goes in v3:
time: 209 us; the launch traced here: 208 us
  Pallas kernels  129 us (62%)
  local copies, waits for them, and re-layouts  32 us (15%)
  matrix products  21.7 us (10%)
  other arithmetic  12.9 us (6%)
  starting transfers between devices  10.8 us (5%)
    pallas_call x1, Pallas kernels, gather_and_scatter(): pl.pallas_call(backward_kernel, out_shape=(jax.ShapeDtypeStruct((size,) +...  79.6 us
    pallas_call x1, Pallas kernels, gather_blocks(): pl.pallas_call(gather_kernel, out_shape=(jax.ShapeDtypeStruct((size,) + b...  49.6 us
    all_to_all x2, starting transfers between devices, edge_rows(): lax.all_to_all(stacked, ('row', 'col'), split_axis=1, concat_axis=1, tile...  10.8 us
    unnamed x87, local copies, waits for them, and re-layouts  10.7 us
    gather x8, local copies, waits for them, and re-layouts, select_rows(): picked = values[jnp.maximum(positions, 0)]  4.83 us
  transfers between devices with their start and end apart: 2, of which 0 were waited for; matrix products, arithmetic and copies ran while one was open for 17% of the time, Pallas kernels for 62%

profile of v3, /device:TPU:0, one launch (start us, length us, event | category | flops | bytes accessed | tf_op | source)
XLA Modules:
  0.0 207.7 jit_solution(10167267673512418601)
XLA Ops:
  3.9 2.0 gather_fusion.1
  7.5 1.0 pad_maximum_fusion.2
  8.5 7.4 %all-to-all-start = ((bf16[2,32,4,768]{3,2,0,1:T(4,128)(2,1)}), bf16[2,32,4,768]{3,2,0,1:T(4,128)(2,1)}, u32[]{:S(2)}, u32[]{:S(2)}) async-start(bf16[2,32,4,768]{3,2,0,1:T(4,128)(2,1)} %pad_maximum_fusion.2), calls=%async_computation | async-start | bytes 786432 | tf_op jit(solution)/shard_map/all_to_all | solution.py:35
  18.1 49.6 %shard_map.164 = (bf16[8,272,768]{2,1,0:T(8,128)(2,1)S(1)}, bf16[256,2048]{1,0:T(8,128)(2,1)S(1)}) custom-call(bf16[272,768]{1,0:T(8,128)(2,1)S(1)} %pad_maximum_fusion.1.block, s32[256,16]{1,0:T(8,128)S(1)} %copy.61.entries), custom_call_target="tpu_custom_call" | custom-call | tf_op jit(solution)/shard_map/pallas_call | solution.py:179
  67.7 1.9 slice.24
  70.4 1.6 fusion.25
  74.5 1.6 fusion.8
  76.1 3.7 %fusion.7 = bf16[256,768]{1,0:T(8,128)(2,1)} fusion(bf16[256,2048]{1,0:T(8,128)(2,1)S(1)} %get-tuple-element.10, bf16[2048,768]{1,0:T(8,128)(2,1)} %bitcast.91, f32[256]{0:T(256)S(1)} %broadcast_maximum_fusion.4), kind=kOutput, calls=%fused_computation.23 | convolution fusion | flops 805699584 | bytes 4588544 | tf_op jit(solution)/shard_map/dot_general | solution.py:388
  80.6 1.9 copy.71
  82.5 1.0 copy.73
  83.5 1.6 copy.78
  85.0 1.8 constant_dynamic-update-slice_fusion.3
  86.8 1.6 fusion.26
  89.6 1.2 fusion.24
  91.5 1.2 fusion
  92.8 1.7 multiply_convert_fusion.1
  94.5 1.4 fusion.2.block
  98.4 1.8 multiply_convert_fusion
  102.4 0.9 copy.72
  103.3 1.9 copy.74
  107.4 1.0 pad_maximum_fusion.3
  108.5 3.4 %all-to-all-start.1 = ((bf16[2,32,4,768]{3,2,0,1:T(4,128)(2,1)}), bf16[2,32,4,768]{3,2,0,1:T(4,128)(2,1)}, u32[]{:S(2)}, u32[]{:S(2)}) async-start(bf16[2,32,4,768]{3,2,0,1:T(4,128)(2,1)} %pad_maximum_fusion.3), calls=%async_computation.1 | async-start | bytes 786432 | tf_op jit(solution)/shard_map/all_to_all | solution.py:35
  111.9 1.8 constant_dynamic-update-slice_fusion.2
  113.7 1.8 constant_dynamic-update-slice_fusion.1
  116.3 1.1 pad_maximum_fusion.right
  117.4 79.6 %shard_map.165 = (bf16[8,256,768]{2,1,0:T(8,128)(2,1)}, f32[5,192,128]{2,1,0:T(8,128)}, bf16[256,2048]{1,0:T(8,128)(2,1)}) custom-call(bf16[256,768]{1,0:T(8,128)(2,1)} %fusion.2.block, bf16[5,4,192,256]{3,2,1,0:T(8,128)(2,1)} %constant_dynamic-update-slice_fusion.left, bf16[2,256,1024]{2,1,0:T(8,128)(2,1)} %pad_maximum_fusion.right, s32[16,2048]{1,0:T(8,128)} %bitcast.100), custom_call_target="tpu_custom_call" | custom-call | tf_op jit(solution)/shard_map/pallas_call | solution.py:332
  197.0 1.9 broadcast_multiply_fusion
  198.8 3.3 %fusion.27 = f32[256,768]{1,0:T(8,128)S(1)} fusion(bf16[256,2048]{1,0:T(8,128)(2,1)} %get-tuple-element.12, bf16[2048,768]{1,0:T(8,128)(2,1)} %bitcast.103), kind=kOutput, calls=%fused_computation.88 | convolution fusion | flops 805306368 | bytes 4980736 | tf_op jit(solution)/shard_map/dot_general | solution.py:428
  202.8 1.8 fusion.23
  204.7 1.0 reshape_squeeze.15
  205.7 1.0 fusion.5
  206.7 1.0 fusion.6
  (131 shorter events, 21.3 us)
Async XLA Ops:
  0.6 92.1 %copy-start = (bf16[768,1024]{1,0:T(8,128)(2,1)S(1)}, bf16[768,1024]{1,0:T(8,128)(2,1)}, u32[]{:S(2)}) copy-start(bf16[768,1024]{1,0:T(8,128)(2,1)} %param.20) | copy-start | bytes 4718596
  0.6 5.5 %copy-start.2 = (bf16[256,768]{1,0:T(8,128)(2,1)S(1)}, bf16[256,768]{1,0:T(8,128)(2,1)}, u32[]{:S(2)}) copy-start(bf16[256,768]{1,0:T(8,128)(2,1)} %param.14) | copy-start | bytes 1179652
  7.0 9.0 %copy-start.20 = (s32[256,16]{0,1:T(8,128)S(1)}, s32[256,16]{0,1:T(8,128)}, u32[]{:S(2)}) copy-start(s32[256,16]{0,1:T(8,128)} %param.15) | copy-start | bytes 49156
  7.0 9.7 %copy-start.23 = (s32[1,32,4]{1,2,0:T(4,128)S(1)}, s32[1,32,4]{1,2,0:T(4,128)}, u32[]{:S(2)}) copy-start(s32[1,32,4]{1,2,0:T(4,128)} %param.17) | copy-start | bytes 1540
  7.0 10.4 %copy-start.24 = (s32[1,32,4]{1,2,0:T(4,128)S(1)}, s32[1,32,4]{1,2,0:T(4,128)}, u32[]{:S(2)}) copy-start(s32[1,32,4]{1,2,0:T(4,128)} %param.16) | copy-start | bytes 1540
  7.0 11.0 %copy-start.1 = (bf16[256,768]{1,0:T(8,128)(2,1)S(1)}, bf16[256,768]{1,0:T(8,128)(2,1)}, u32[]{:S(2)}) copy-start(bf16[256,768]{1,0:T(8,128)(2,1)} %param.13) | copy-start | bytes 1179652
  8.5 81.0 %all-to-all-start = ((bf16[2,32,4,768]{3,2,0,1:T(4,128)(2,1)}), bf16[2,32,4,768]{3,2,0,1:T(4,128)(2,1)}, u32[]{:S(2)}, u32[]{:S(2)}) async-start(bf16[2,32,4,768]{3,2,0,1:T(4,128)(2,1)} %pad_maximum_fusion.2), calls=%async_computation | async-start | bytes 786432 | tf_op jit(solution)/shard_map/all_to_all | solution.py:35
  67.7 2.7 %copy-start.3 = (bf16[768,1024]{1,0:T(8,128)(2,1)S(1)}, bf16[768,1024]{1,0:T(8,128)(2,1)}, u32[]{:S(2)}) copy-start(bf16[768,1024]{1,0:T(8,128)(2,1)} %param.18) | copy-start | bytes 4718596
  70.4 1.6 copy-start.22
  70.4 2.4 %copy-start.21 = (s32[1,32,4]{2,1,0:T(8,128)S(1)}, s32[1,32,4]{2,1,0:T(8,128)}, u32[]{:S(2)}) copy-start(s32[1,32,4]{2,1,0:T(8,128)} %copy.69) | copy-start | bytes 1540
  72.0 7.8 %copy-start.33 = (f32[256]{0:T(256)}, f32[256]{0:T(256)S(1)}, u32[]{:S(2)}) copy-start(f32[256]{0:T(256)S(1)} %broadcast_maximum_fusion.4) | copy-start | bytes 3076
  72.1 7.7 %copy-start.26 = (s32[128]{0:T(128)}, s32[128]{0:T(128)S(1)}, u32[]{:S(2)}) copy-start(s32[128]{0:T(128)S(1)} %eq.30) | copy-start | bytes 1540
  72.9 6.9 %copy-start.29 = (s32[128]{0:T(128)}, s32[128]{0:T(128)S(1)}, u32[]{:S(2)}) copy-start(s32[128]{0:T(128)S(1)} %eq.34) | copy-start | bytes 1540
  76.1 3.7 %copy-start.14 = (bf16[768,256]{1,0:T(8,128)(2,1)S(1)}, bf16[768,256]{1,0:T(8,128)(2,1)}, u32[]{:S(2)}) copy-start(bf16[768,256]{1,0:T(8,128)(2,1)} %copy.70) | copy-start | bytes 1179652
  79.8 7.0 %copy-start.5 = (bf16[768,1024]{1,0:T(8,128)(2,1)S(1)}, bf16[768,1024]{1,0:T(8,128)(2,1)}, u32[]{:S(2)}) copy-start(bf16[768,1024]{1,0:T(8,128)(2,1)} %param.21) | copy-start | bytes 4718596
  86.8 2.1 %copy-start.15 = (bf16[768,1024]{1,0:T(8,128)(2,1)S(1)}, bf16[768,1024]{1,0:T(8,128)(2,1)}, u32[]{:S(2)}) copy-start(bf16[768,1024]{1,0:T(8,128)(2,1)} %param.19) | copy-start | bytes 4718596
  86.8 2.2 %copy-start.17 = (bf16[256,768]{1,0:T(8,128)(2,1)S(1)}, bf16[256,768]{1,0:T(8,128)(2,1)}, u32[]{:S(2)}) copy-start(bf16[256,768]{1,0:T(8,128)(2,1)} %fusion.7) | copy-start | bytes 1179652
  89.0 2.5 %copy-start.27 = (s32[128]{0:T(128)S(1)}, s32[128]{0:T(128)}, u32[]{:S(2)}) copy-start(s32[128]{0:T(128)} %copy-done.26) | copy-start | bytes 1540
  89.0 2.5 %copy-start.35 = (f32[256]{0:T(256)S(1)}, f32[256]{0:T(256)}, u32[]{:S(2)}) copy-start(f32[256]{0:T(256)} %broadcast_maximum_fusion.3) | copy-start | bytes 3076
  92.7 1.7 copy-start.16
  92.7 1.7 copy-start.34
  96.6 1.8 copy-start.37
  98.4 1.8 copy-start.19
  100.2 1.6 copy-start.6
  108.5 7.8 %copy-start.9 = (bf16[256,1024]{1,0:T(8,128)(2,1)S(1)}, bf16[256,1024]{1,0:T(8,128)(2,1)}, u32[]{:S(2)}) copy-start(bf16[256,1024]{1,0:T(8,128)(2,1)} %copy-done.8) | copy-start | bytes 1572868
  108.5 7.8 %copy-start.12 = (bf16[256,1024]{1,0:T(8,128)(2,1)S(1)}, bf16[256,1024]{1,0:T(8,128)(2,1)}, u32[]{:S(2)}) copy-start(bf16[256,1024]{1,0:T(8,128)(2,1)} %copy-done.11) | copy-start | bytes 1572868
  108.5 94.4 %all-to-all-start.1 = ((bf16[2,32,4,768]{3,2,0,1:T(4,128)(2,1)}), bf16[2,32,4,768]{3,2,0,1:T(4,128)(2,1)}, u32[]{:S(2)}, u32[]{:S(2)}) async-start(bf16[2,32,4,768]{3,2,0,1:T(4,128)(2,1)} %pad_maximum_fusion.3), calls=%async_computation.1 | async-start | bytes 786432 | tf_op jit(solution)/shard_map/all_to_all | solution.py:35
  111.9 3.6 %copy-start.13 = (bf16[768,256]{1,0:T(8,128)(2,1)S(1)}, bf16[768,256]{1,0:T(8,128)(2,1)}, u32[]{:S(2)}) copy-start(bf16[768,256]{1,0:T(8,128)(2,1)} %copy.74) | copy-start | bytes 1179652
  198.8 3.3 %copy-start.4 = (bf16[768,1024]{1,0:T(8,128)(2,1)S(1)}, bf16[768,1024]{1,0:T(8,128)(2,1)}, u32[]{:S(2)}) copy-start(bf16[768,1024]{1,0:T(8,128)(2,1)} %param.18) | copy-start | bytes 4718596
  198.8 3.3 %copy-start.10 = (bf16[256,1024]{1,0:T(8,128)(2,1)S(1)}, bf16[256,1024]{1,0:T(8,128)(2,1)}, u32[]{:S(2)}) copy-start(bf16[256,1024]{1,0:T(8,128)(2,1)} %copy-done.8) | copy-start | bytes 1572868
  202.8 2.9 %copy-start.28 = (s32[128]{0:T(128)S(1)}, s32[128]{0:T(128)}, u32[]{:S(2)}) copy-start(s32[128]{0:T(128)} %copy-done.26) | copy-start | bytes 1540
  202.8 3.9 %copy-start.31 = (s32[128]{0:T(128)S(1)}, s32[128]{0:T(128)}, u32[]{:S(2)}) copy-start(s32[128]{0:T(128)} %copy-done.29) | copy-start | bytes 1540
  (10 other events, 11.8 us)

commit v4 on v3

--- a/solution.py
+++ b/solution.py
@@ -1,3 +1,5 @@
+import functools
+
 import jax
 import jax.numpy as jnp
 from jax import lax
@@ -199,9 +201,10 @@
     return counts
 
 
-def backward_kernel(
-    block, left, right, entries, got, total, table, up, down, cross, landed, sent, heard, acc_rows, acc, *buffers
-):
+def backward_kernel(matrices, block, entries, *refs):
+    lefts, rights = refs[:matrices], refs[matrices : matrices + 2]
+    got, total, table, up, down, cross, landed, sent, heard = refs[matrices + 2 : matrices + 11]
+    acc_rows, acc, *buffers = refs[matrices + 11 :]
     line = Line(block, got, up, down, cross, landed)
     row_stages = axis_bits("row")
     stages = row_stages + axis_bits("col")
@@ -209,12 +212,12 @@
     line.first()
     count = len(stages)
     send_buf, recv_buf = buffers[:count], buffers[count:]
-    matrices, rows = left.shape[:2]
+    rows = lefts[0].shape[0]
     each = block.shape[0]
 
     def product(matrix, at):
         return jnp.dot(
-            left[matrix, at], right[matrix // 3], preferred_element_type=jnp.float32
+            lefts[matrix][at], rights[matrix // 3][...], preferred_element_type=jnp.float32
         )
 
     columns = lax.axis_size("col")
@@ -233,8 +236,8 @@
 
     mine = lax.axis_index("row") % 2
 
-    @pl.loop(0, matrices)
-    def _(matrix):
+    for matrix in range(matrices):
+
         @pl.loop(0, rows // 2)
         def _(k):
             send_buf[0][matrix, k] = product(matrix, 2 * k + 1 - mine).astype(jnp.bfloat16)
@@ -320,23 +323,24 @@
     line.finish()
 
 
-def gather_and_scatter(block, left, right, entries):
+def gather_and_scatter(block, lefts, rights, entries):
     rows, size = lax.axis_size("row"), lax.axis_size("col")
-    matrices, depth, each = left.shape
-    wide = right.shape[2]
+    matrices = len(lefts)
+    depth, each = lefts[0].shape
+    wide = rights[0].shape[1]
     high, width = depth // rows, wide // size
     buffers = [
         pltpu.VMEM((matrices, n, high, wide), jnp.bfloat16) for n in halving_counts(rows)
     ] + [pltpu.VMEM((matrices, n, high, width), jnp.bfloat16) for n in halving_counts(size)]
     vmem = pl.BlockSpec(memory_space=pltpu.VMEM)
     return pl.pallas_call(
-        backward_kernel,
+        functools.partial(backward_kernel, matrices),
         out_shape=(
             jax.ShapeDtypeStruct((size,) + block.shape, block.dtype),
             jax.ShapeDtypeStruct((matrices, high, width), jnp.float32),
             jax.ShapeDtypeStruct((block.shape[0], entries.shape[1]), jnp.bfloat16),
         ),
-        in_specs=[vmem] * 4,
+        in_specs=[vmem] * (2 + matrices + len(rights)),
         out_specs=(vmem,) * 3,
         scratch_shapes=line_semaphores()
         + [pltpu.SemaphoreType.DMA((len(buffers), matrices)) for _ in range(2)]
@@ -349,7 +353,7 @@
         compiler_params=pltpu.CompilerParams(
             collective_id=1, has_side_effects=True, vmem_limit_bytes=56 * 2**20
         ),
-    )(block, left.reshape(matrices, rows, high, each), right, entries)
+    )(block, entries, *[left.reshape(rows, high, each) for left in lefts], *rights)
 
 
 def listed_rows(entries, width):
@@ -421,9 +425,9 @@
     dz_cite = (project_back(dpre_paper, w_cite) / cnt_cite).astype(jnp.bfloat16)
     dz_write = (project_back(dpre_paper, w_write) / cnt_write).astype(jnp.bfloat16)
     dz_written = (project_back(dpre_author, w_written) / cnt_written).astype(jnp.bfloat16)
-    left_sides = jnp.stack([x_paper.T, cited.T, written.T, x_author.T, authored.T])
+    left_sides = [x_paper.T, cited.T, written.T, x_author.T, authored.T]
     dz_rows, summed, table_cited = gather_and_scatter(
-        dz_cite, left_sides, jnp.stack([dpre_paper, dpre_author]), entries
+        dz_cite, left_sides, [dpre_paper, dpre_author], entries
     )
     cite_grad = jnp.dot(
         table_cited, dz_rows.reshape(-1, width), preferred_element_type=jnp.float32

time: 209 us -> 206 us (0.986)
  local copies, waits for them, and re-layouts: 32 us -> 23.4 us
  Pallas kernels: 129 us -> 136 us
    unnamed x87 -> x71, local copies, waits for them, and re-layouts: 10.7 us -> 3.84 us
    pallas_call x1, Pallas kernels: 79.6 us -> 86.1 us  [gather_and_scatter(): pl.pallas_call(functools.partial(backward_kernel, matrices), out_shape=(j...]
  transfers between devices with their start and end apart: 2 -> 2, of which waited for: 0 -> 0; matrix products, arithmetic and copies ran while one was open for 17% -> 13% of each run, Pallas kernels for 62% -> 66%
where the time goes in v4:
time: 206 us
  Pallas kernels  136 us (66%)
  local copies, waits for them, and re-layouts  23.4 us (11%)
  matrix products  22.8 us (11%)
  other arithmetic  12.5 us (6%)
  starting transfers between devices  10 us (5%)
    pallas_call x1, Pallas kernels, gather_and_scatter(): pl.pallas_call(functools.partial(backward_kernel, matrices), out_shape=(j...  86.1 us
    pallas_call x1, Pallas kernels, gather_blocks(): pl.pallas_call(gather_kernel, out_shape=(jax.ShapeDtypeStruct((size,) + b...  49.6 us
    all_to_all x2, starting transfers between devices, edge_rows(): lax.all_to_all(stacked, ('row', 'col'), split_axis=1, concat_axis=1, tile...  10 us
    gather x8, local copies, waits for them, and re-layouts, select_rows(): picked = values[jnp.maximum(positions, 0)]  4.83 us
  transfers between devices with their start and end apart: 2, of which 0 were waited for; matrix products, arithmetic and copies ran while one was open for 13% of the time, Pallas kernels for 66%

profile of v4, /device:TPU:0, one launch (start us, length us, event | category | flops | bytes accessed | tf_op | source)
XLA Modules:
  0.0 205.5 jit_solution(2899966782056011508)
XLA Ops:
  3.7 2.0 gather_fusion.1
  6.1 0.9 gather_fusion
  7.5 1.0 pad_maximum_fusion.1
  8.5 7.4 %all-to-all-start = ((bf16[2,32,4,768]{3,2,0,1:T(4,128)(2,1)}), bf16[2,32,4,768]{3,2,0,1:T(4,128)(2,1)}, u32[]{:S(2)}, u32[]{:S(2)}) async-start(bf16[2,32,4,768]{3,2,0,1:T(4,128)(2,1)} %pad_maximum_fusion.1), calls=%async_computation | async-start | bytes 786432 | tf_op jit(solution)/shard_map/all_to_all | solution.py:37
  18.1 49.6 %shard_map.164 = (bf16[8,272,768]{2,1,0:T(8,128)(2,1)S(1)}, bf16[256,2048]{1,0:T(8,128)(2,1)S(1)}) custom-call(bf16[272,768]{1,0:T(8,128)(2,1)S(1)} %pad_maximum_fusion.block, s32[256,16]{1,0:T(8,128)S(1)} %copy.61.entries), custom_call_target="tpu_custom_call" | custom-call | tf_op jit(solution)/shard_map/pallas_call | solution.py:181
  67.7 1.8 slice.24
  70.3 1.6 fusion.25
  73.5 1.0 fusion.8
  75.2 0.9 copy.71
  76.1 3.6 %fusion.7 = bf16[256,768]{1,0:T(8,128)(2,1)} fusion(bf16[256,2048]{1,0:T(8,128)(2,1)S(1)} %get-tuple-element.10, bf16[2048,768]{1,0:T(8,128)(2,1)} %bitcast.89, f32[256]{0:T(256)S(1)} %broadcast_maximum_fusion.4), kind=kOutput, calls=%fused_computation.23 | convolution fusion | flops 805699584 | bytes 4588544 | tf_op jit(solution)/shard_map/dot_general | solution.py:392
  79.7 2.0 copy.72
  81.7 0.9 copy.74
  82.7 1.4 broadcast_maximum_fusion.2
  84.1 1.5 fusion.26
  86.2 1.2 fusion.24
  88.1 1.2 fusion
  89.4 1.7 multiply_convert_fusion.1
  91.1 1.4 fusion.2.block
  93.5 0.9 copy-done.14
  95.0 2.9 %multiply_convert_fusion = (bf16[256,1024]{1,0:T(8,128)(2,1)S(1)}, bf16[256,1024]{1,0:T(8,128)(2,1)}) fusion(bf16[256,1024]{1,0:T(8,128)(2,1)} %param.24, f32[256,1024]{1,0:T(8,128)S(1)} %copy-done.14, bf16[256,768]{1,0:T(8,128)(2,1)S(1)} %fusion.1, bf16[768,1024]{1,0:T(8,128)(2,1)S(1)} %copy-done.32), kind=kOutput, calls=%fused_computation.24 | convolution fusion | flops 406061056 | bytes 4587520 | tf_op jit(solution)/shard_map/dot_general | solution.py:418
  100.1 0.9 copy.73
  101.0 1.9 copy.75
  105.1 1.0 pad_maximum_fusion.2
  106.1 2.6 %all-to-all-start.1 = ((bf16[2,32,4,768]{3,2,0,1:T(4,128)(2,1)}), bf16[2,32,4,768]{3,2,0,1:T(4,128)(2,1)S(1)}, u32[]{:S(2)}, u32[]{:S(2)}) async-start(bf16[2,32,4,768]{3,2,0,1:T(4,128)(2,1)} %pad_maximum_fusion.2), calls=%async_computation.1 | async-start | bytes 786432 | tf_op jit(solution)/shard_map/all_to_all | solution.py:37
  108.7 86.1 %shard_map.165 = (bf16[8,256,768]{2,1,0:T(8,128)(2,1)}, f32[5,192,128]{2,1,0:T(8,128)}, bf16[256,2048]{1,0:T(8,128)(2,1)}) custom-call(bf16[256,768]{1,0:T(8,128)(2,1)} %fusion.2.block, s32[16,2048]{1,0:T(8,128)} %bitcast.96, bf16[4,192,256]{2,1,0:T(8,128)(2,1)} %bitcast.90, bf16[4,192,256]{2,1,0:T(8,128)(2,1)} %bitcast.91, bf16[4,192,256]{2,1,0:T(8,128)(2,1)} %bitcast.93, ...), custom_call_target="tpu_custom_call" | custom-call | tf_op jit(solution)/shard_map/pallas_call | solution.py:336
  194.8 1.9 broadcast_multiply_fusion
  196.7 3.3 %fusion.27 = f32[256,768]{1,0:T(8,128)S(1)} fusion(bf16[256,2048]{1,0:T(8,128)(2,1)} %get-tuple-element.12, bf16[2048,768]{1,0:T(8,128)(2,1)} %bitcast.99), kind=kOutput, calls=%fused_computation.82 | convolution fusion | flops 805306368 | bytes 4980736 | tf_op jit(solution)/shard_map/dot_general | solution.py:432
  200.7 0.9 fusion.23
  201.5 1.0 reshape_squeeze.14
  202.5 1.0 reshape_squeeze.15
  203.5 1.0 fusion.5
  204.5 1.0 fusion.6
  (113 shorter events, 16.9 us)
Async XLA Ops:
  0.6 88.7 %copy-start = (bf16[768,1024]{1,0:T(8,128)(2,1)S(1)}, bf16[768,1024]{1,0:T(8,128)(2,1)}, u32[]{:S(2)}) copy-start(bf16[768,1024]{1,0:T(8,128)(2,1)} %param.20) | copy-start | bytes 4718596
  0.6 5.5 %copy-start.2 = (bf16[256,768]{1,0:T(8,128)(2,1)S(1)}, bf16[256,768]{1,0:T(8,128)(2,1)}, u32[]{:S(2)}) copy-start(bf16[256,768]{1,0:T(8,128)(2,1)} %param.14) | copy-start | bytes 1179652
  7.0 8.9 %copy-start.16 = (s32[256,16]{0,1:T(8,128)S(1)}, s32[256,16]{0,1:T(8,128)}, u32[]{:S(2)}) copy-start(s32[256,16]{0,1:T(8,128)} %param.15) | copy-start | bytes 49156
  7.0 9.6 %copy-start.19 = (s32[1,32,4]{1,2,0:T(4,128)S(1)}, s32[1,32,4]{1,2,0:T(4,128)}, u32[]{:S(2)}) copy-start(s32[1,32,4]{1,2,0:T(4,128)} %param.17) | copy-start | bytes 1540
  7.0 10.3 %copy-start.20 = (s32[1,32,4]{1,2,0:T(4,128)S(1)}, s32[1,32,4]{1,2,0:T(4,128)}, u32[]{:S(2)}) copy-start(s32[1,32,4]{1,2,0:T(4,128)} %param.16) | copy-start | bytes 1540
  7.0 11.0 %copy-start.1 = (bf16[256,768]{1,0:T(8,128)(2,1)S(1)}, bf16[256,768]{1,0:T(8,128)(2,1)}, u32[]{:S(2)}) copy-start(bf16[256,768]{1,0:T(8,128)(2,1)} %param.13) | copy-start | bytes 1179652
  8.5 77.7 %all-to-all-start = ((bf16[2,32,4,768]{3,2,0,1:T(4,128)(2,1)}), bf16[2,32,4,768]{3,2,0,1:T(4,128)(2,1)}, u32[]{:S(2)}, u32[]{:S(2)}) async-start(bf16[2,32,4,768]{3,2,0,1:T(4,128)(2,1)} %pad_maximum_fusion.1), calls=%async_computation | async-start | bytes 786432 | tf_op jit(solution)/shard_map/all_to_all | solution.py:37
  67.7 2.6 %copy-start.3 = (bf16[768,1024]{1,0:T(8,128)(2,1)S(1)}, bf16[768,1024]{1,0:T(8,128)(2,1)}, u32[]{:S(2)}) copy-start(bf16[768,1024]{1,0:T(8,128)(2,1)} %param.18) | copy-start | bytes 4718596
  70.3 1.6 copy-start.21
  70.3 1.6 copy-start.18
  70.3 2.4 %copy-start.17 = (s32[1,32,4]{2,1,0:T(8,128)S(1)}, s32[1,32,4]{2,1,0:T(8,128)}, u32[]{:S(2)}) copy-start(s32[1,32,4]{2,1,0:T(8,128)} %copy.69) | copy-start | bytes 1540
  71.9 4.2 %copy-start.28 = (f32[256]{0:T(256)}, f32[256]{0:T(256)S(1)}, u32[]{:S(2)}) copy-start(f32[256]{0:T(256)S(1)} %broadcast_maximum_fusion.4) | copy-start | bytes 3076
  72.0 4.1 %copy-start.22 = (s32[128]{0:T(128)}, s32[128]{0:T(128)S(1)}, u32[]{:S(2)}) copy-start(s32[128]{0:T(128)S(1)} %eq.30) | copy-start | bytes 1540
  72.8 3.3 %copy-start.25 = (s32[128]{0:T(128)}, s32[128]{0:T(128)S(1)}, u32[]{:S(2)}) copy-start(s32[128]{0:T(128)S(1)} %eq.34) | copy-start | bytes 1540
  79.7 4.4 %copy-start.5 = (bf16[768,1024]{1,0:T(8,128)(2,1)S(1)}, bf16[768,1024]{1,0:T(8,128)(2,1)}, u32[]{:S(2)}) copy-start(bf16[768,1024]{1,0:T(8,128)(2,1)} %param.21) | copy-start | bytes 4718596
  82.7 3.0 %copy-start.7 = (f32[256,1024]{1,0:T(8,128)S(1)}, f32[256,1024]{1,0:T(8,128)}, u32[]{:S(2)}) copy-start(f32[256,1024]{1,0:T(8,128)} %fusion.25) | copy-start | bytes 3145732
  82.7 3.0 %copy-start.11 = (bf16[768,1024]{1,0:T(8,128)(2,1)S(1)}, bf16[768,1024]{1,0:T(8,128)(2,1)}, u32[]{:S(2)}) copy-start(bf16[768,1024]{1,0:T(8,128)(2,1)} %param.19) | copy-start | bytes 4718596
  82.7 3.0 %copy-start.13 = (bf16[256,768]{1,0:T(8,128)(2,1)S(1)}, bf16[256,768]{1,0:T(8,128)(2,1)}, u32[]{:S(2)}) copy-start(bf16[256,768]{1,0:T(8,128)(2,1)} %fusion.7) | copy-start | bytes 1179652
  85.6 2.5 %copy-start.23 = (s32[128]{0:T(128)S(1)}, s32[128]{0:T(128)}, u32[]{:S(2)}) copy-start(s32[128]{0:T(128)} %copy-done.22) | copy-start | bytes 1540
  85.6 2.5 %copy-start.30 = (f32[256]{0:T(256)S(1)}, f32[256]{0:T(256)}, u32[]{:S(2)}) copy-start(f32[256]{0:T(256)} %broadcast_maximum_fusion.3) | copy-start | bytes 3076
  88.1 1.3 copy-start.33
  89.4 1.7 copy-start.12
  89.4 1.7 copy-start.29
  91.1 1.4 copy-start.8
  93.2 1.7 copy-start.32
  95.0 2.9 %copy-start.15 = (bf16[256,768]{1,0:T(8,128)(2,1)}, bf16[256,768]{1,0:T(8,128)(2,1)S(1)}, u32[]{:S(2)}) copy-start(bf16[256,768]{1,0:T(8,128)(2,1)S(1)} %fusion.1) | copy-start | bytes 1179652
  97.9 1.6 copy-start.6
  106.1 94.5 %all-to-all-start.1 = ((bf16[2,32,4,768]{3,2,0,1:T(4,128)(2,1)}), bf16[2,32,4,768]{3,2,0,1:T(4,128)(2,1)S(1)}, u32[]{:S(2)}, u32[]{:S(2)}) async-start(bf16[2,32,4,768]{3,2,0,1:T(4,128)(2,1)} %pad_maximum_fusion.2), calls=%async_computation.1 | async-start | bytes 786432 | tf_op jit(solution)/shard_map/all_to_all | solution.py:37
  196.6 3.3 %copy-start.4 = (bf16[768,1024]{1,0:T(8,128)(2,1)S(1)}, bf16[768,1024]{1,0:T(8,128)(2,1)}, u32[]{:S(2)}) copy-start(bf16[768,1024]{1,0:T(8,128)(2,1)} %param.18) | copy-start | bytes 4718596
  196.6 3.4 %copy-start.9 = (bf16[256,1024]{1,0:T(8,128)(2,1)S(1)}, bf16[256,1024]{1,0:T(8,128)(2,1)}, u32[]{:S(2)}) copy-start(bf16[256,1024]{1,0:T(8,128)(2,1)} %copy-done.8) | copy-start | bytes 1572868
  200.6 2.9 %copy-start.24 = (s32[128]{0:T(128)S(1)}, s32[128]{0:T(128)}, u32[]{:S(2)}) copy-start(s32[128]{0:T(128)} %copy-done.22) | copy-start | bytes 1540
  200.6 3.9 %copy-start.27 = (s32[128]{0:T(128)S(1)}, s32[128]{0:T(128)}, u32[]{:S(2)}) copy-start(s32[128]{0:T(128)} %copy-done.25) | copy-start | bytes 1540
  (4 other events, 3.5 us)
